TPU v7x, 32 devices: a whole 2x2x4 slice. The times are simulated.
32 devices in a mesh: ctx: 16 (over z, y, core), hg: 2 (over x).
Axes of the slice: x: 2, y: 2, z: 4, core: 2. Of those that a mesh axis runs over, the one named last changes fastest.
Arguments:
- query_latent_plain: bfloat16 [2048, 32, 512], P('ctx', 'hg'), may hold values from -40 to 40
- query_rope: bfloat16 [2048, 32, 64], P('ctx', 'hg'), may hold values from -40 to 40
- latent_nope: bfloat16 [2048, 512], P('ctx'), may hold values from -6 to 6
- latent_rope: bfloat16 [2048, 64], P('ctx'), may hold values from -6 to 6
- latent_output_gradient: bfloat16 [2048, 32, 512], P('ctx', 'hg'), may hold values from -5 to 5
- block_mask: int32 [32, 32], replicated, may hold values from 0 to 1, as said below
Outputs:
- d_query_nope: bfloat16 [2048, 32, 512], P('ctx', 'hg')
- d_query_rope: bfloat16 [2048, 32, 64], P('ctx', 'hg')
- d_latent_nope: float32 [2048, 512], P(('ctx', 'hg'))
- d_latent_rope: float32 [2048, 64], P(('ctx', 'hg'))
Inputs may be any that keep to these rules, and one draw needn't show every extreme that they name: Every mask block may attend to itself: block_mask[b, b] = 1.
All inputs are finite; a program needn't handle non-finite values.
Results may differ from a plain program's by a relative error of at most 0.012.
Values may be sent and summed in bfloat16 or wider, within the bound.
A program may use at most 64 MiB of HBM per device.

v0:
```python
import jax
import jax.numpy as jnp
from jax import lax
from jax.sharding import PartitionSpec as P

WINDOW = 4


SCORE_SCALE = 192.0 ** (-0.5)


def from_behind(block, axis, distance):
    devices = range(lax.axis_size(axis))
    route = [((i - distance) % len(devices), i) for i in devices]
    return lax.ppermute(block, axis, route)


def for_sending(shard):
    return jax.tree.map(lambda a: a.astype(jnp.bfloat16) if a.dtype == jnp.float32 else a, shard)


def allowed_tile(block_mask, me_cycle, source, row_count, head_total, keys):
    tile = lax.dynamic_slice(block_mask, (2 * me_cycle, 2 * source), (2, 2))
    half = keys // 2
    row_half = lax.broadcasted_iota(jnp.int32, (row_count, 1), 0) // head_total // half
    key_half = lax.broadcasted_iota(jnp.int32, (1, keys), 1) // half
    upper = jnp.where(key_half == 0, tile[0, 0], tile[0, 1])
    lower = jnp.where(key_half == 0, tile[1, 0], tile[1, 1])
    return jnp.where(row_half == 0, upper, lower) == 1


def on_device(
    query_latent_plain, query_rope, latent_nope, latent_rope, latent_output_gradient, block_mask
):
    token_total, head_total, latent_width = query_latent_plain.shape
    rope = query_rope.shape[2]
    row_count = token_total * head_total
    me_cycle = lax.axis_index("ctx")
    cycle_size = lax.axis_size("ctx")
    query_plain = query_latent_plain.reshape(row_count, latent_width)
    q_rope = query_rope.reshape(row_count, rope)
    output_gradient_rows = latent_output_gradient.reshape(row_count, latent_width)
    current = (latent_nope, latent_rope)
    held = []
    masked_list = []
    dprob_list = []
    run_max = jnp.full((row_count,), -1e30, jnp.float32)
    run_sum = jnp.zeros((row_count,), jnp.float32)
    run_dot = jnp.zeros((row_count,), jnp.float32)
    for step in range(WINDOW):
        if step > 0:
            current = from_behind((current[0], current[1]), "ctx", 1)
        held.append(current)
        source = (me_cycle - step) % cycle_size
        allowed = allowed_tile(block_mask, me_cycle, source, row_count, head_total, token_total)
        scores = (
            jnp.einsum("rd,kd->rk", query_plain, current[0], preferred_element_type=jnp.float32)
            + jnp.einsum("rd,kd->rk", q_rope, current[1], preferred_element_type=jnp.float32)
        ) * SCORE_SCALE
        masked = jnp.where(allowed, scores, -jnp.inf)
        new_max = jnp.maximum(run_max, jnp.max(masked, axis=1))
        weights = jnp.exp(masked - new_max[:, None])
        dprob = jnp.einsum(
            "rd,kd->rk", output_gradient_rows, current[0], preferred_element_type=jnp.float32
        )
        fade = jnp.exp(run_max - new_max)
        run_sum = run_sum * fade + jnp.sum(weights, axis=1)
        run_dot = run_dot * fade + jnp.sum(weights * dprob, axis=1)
        run_max = new_max
        masked_list.append(masked)
        dprob_list.append(dprob)
    lse = run_max + jnp.log(run_sum)
    delta = run_dot / run_sum
    query_plain_gradient = jnp.zeros((row_count, latent_width), jnp.float32)
    query_rotary_gradient = jnp.zeros((row_count, rope), jnp.float32)
    carried = None
    for step in range(WINDOW):
        k_nope, k_rope = held[step]
        prob = jnp.exp(masked_list[step] - lse[:, None])
        dscore = (prob * (dprob_list[step] - delta[:, None])).astype(jnp.bfloat16)
        prob_low = prob.astype(jnp.bfloat16)
        query_plain_gradient = query_plain_gradient + SCORE_SCALE * jnp.dot(
            dscore, k_nope, preferred_element_type=jnp.float32
        )
        query_rotary_gradient = query_rotary_gradient + SCORE_SCALE * jnp.dot(
            dscore, k_rope, preferred_element_type=jnp.float32
        )
        dk_nope = SCORE_SCALE * jnp.einsum(
            "rk,rd->kd", dscore, query_plain, preferred_element_type=jnp.float32
        ) + jnp.einsum(
            "rk,rd->kd", prob_low, output_gradient_rows, preferred_element_type=jnp.float32
        )
        dk_rope = SCORE_SCALE * jnp.einsum(
            "rk,rd->kd", dscore, q_rope, preferred_element_type=jnp.float32
        )
        if step == 0:
            carried = (dk_nope, dk_rope)
        else:
            moved = from_behind(carried, "ctx", 1)
            carried = (moved[0] + dk_nope, moved[1] + dk_rope)
    homed = jax.tree.map(
        lambda part, own: part.astype(own.dtype),
        from_behind(for_sending(carried), "ctx", 1 - WINDOW),
        carried,
    )
    plain_gradient, rotary_gradient = jax.tree.map(
        lambda part: part.astype(jnp.float32),
        lax.psum_scatter(for_sending(homed), "hg", scatter_dimension=0, tiled=True),
    )
    return (
        query_plain_gradient.astype(jnp.bfloat16).reshape(token_total, head_total, latent_width),
        query_rotary_gradient.astype(jnp.bfloat16).reshape(token_total, head_total, rope),
        plain_gradient,
        rotary_gradient,
    )


def solution(mesh):
    in_specs = (
        P("ctx", "hg", None),
        P("ctx", "hg", None),
        P("ctx", None),
        P("ctx", None),
        P("ctx", "hg", None),
        P(),
    )
    out_specs = (
        P("ctx", "hg", None),
        P("ctx", "hg", None),
        P(("ctx", "hg"), None),
        P(("ctx", "hg"), None),
    )
    return jax.shard_map(
        on_device, mesh=mesh, in_specs=in_specs, out_specs=out_specs, check_vma=False
    )
```

profile of v0, /device:TPU:0, one launch (start us, length us, event | category | flops | bytes accessed | tf_op | source)
XLA Modules:
  0.0 122.0 jit_solution(12355738562928997981)
XLA Ops:
  7.7 2.6 %collective-permute-start = (bf16[128,512]{1,0:T(8,128)(2,1)}, bf16[128,512]{1,0:T(8,128)(2,1)S(1)}, u32[]{:S(2)}, u32[]{:S(2)}) collective-permute-start(bf16[128,512]{1,0:T(8,128)(2,1)} %param.8), channel_id=1, source_target_pairs={{30,0},{0,2},{2,4},{4,6},{6,8},{8,10},{10,12},{12,14},{14,16},{16,... | collective-permute-start | bytes 393224 | tf_op jit(solution)/shard_map/ppermute | solution.py:15
  10.4 1.4 %copy.16 = bf16[128,16,64]{2,1,0:T(8,128)(2,1)S(1)} copy(bf16[128,16,64]{0,2,1:T(8,128)(2,1)} %param.7) | data formatting | bytes 524288 | tf_op args[1]
  11.8 3.4 %fusion.50 = f32[2048,128]{0,1:T(8,128)} fusion(bf16[2048,512]{1,0:T(8,128)(2,1)} %bitcast.90, bf16[128,512]{1,0:T(8,128)(2,1)} %param.8), kind=kOutput, calls=%fused_computation.115 | convolution fusion | flops 268435456 | bytes 3276800 | tf_op jit(solution)/shard_map/rd,kd->rk/dot_general | solution.py:57
  15.1 0.9 fusion.41
  16.7 1.3 %broadcast_select_fusion.7 = s32[128]{0:T(128)S(1)} fusion(s32[]{:T(128)} %bitcast.1, s32[]{:T(128)} %bitcast), kind=kLoop, calls=%fused_computation.103 | loop fusion | flops 1280 | bytes 520 | tf_op jit(solution)/shard_map/jit(_where)/select_n | solution.py:27
  17.9 1.3 %broadcast_select_fusion.6 = s32[128]{0:T(128)S(1)} fusion(s32[]{:T(128)} %bitcast.3, s32[]{:T(128)} %bitcast.2), kind=kLoop, calls=%fused_computation.102 | loop fusion | flops 1280 | bytes 520 | tf_op jit(solution)/shard_map/jit(_where)/select_n | solution.py:28
  19.2 1.2 %broadcast_select_fusion.5 = s32[128]{0:T(128)S(1)} fusion(s32[]{:T(128)} %bitcast.7, s32[]{:T(128)} %bitcast.6), kind=kLoop, calls=%fused_computation.101 | loop fusion | flops 1280 | bytes 520 | tf_op jit(solution)/shard_map/jit(_where)/select_n | solution.py:27
  20.5 1.3 %broadcast_select_fusion.4 = s32[128]{0:T(128)S(1)} fusion(s32[]{:T(128)} %bitcast.9, s32[]{:T(128)} %bitcast.8), kind=kLoop, calls=%fused_computation.100 | loop fusion | flops 1280 | bytes 520 | tf_op jit(solution)/shard_map/jit(_where)/select_n | solution.py:28
  22.3 1.3 %broadcast_select_fusion.1 = s32[128]{0:T(128)S(1)} fusion(s32[]{:T(128)} %bitcast.15, s32[]{:T(128)} %bitcast.14), kind=kLoop, calls=%fused_computation.97 | loop fusion | flops 1280 | bytes 520 | tf_op jit(solution)/shard_map/jit(_where)/select_n | solution.py:27
  23.6 1.3 %broadcast_select_fusion = s32[128]{0:T(128)S(1)} fusion(s32[]{:T(128)} %bitcast.17, s32[]{:T(128)} %bitcast.16), kind=kLoop, calls=%fused_computation.96 | loop fusion | flops 1280 | bytes 520 | tf_op jit(solution)/shard_map/jit(_where)/select_n | solution.py:28
  24.9 1.2 %broadcast_select_fusion.3 = s32[128]{0:T(128)S(1)} fusion(s32[]{:T(128)} %bitcast.11, s32[]{:T(128)} %bitcast.10), kind=kLoop, calls=%fused_computation.99 | loop fusion | flops 1280 | bytes 520 | tf_op jit(solution)/shard_map/jit(_where)/select_n | solution.py:27
  26.2 1.7 %fusion.49 = (f32[2048]{0:T(1024)S(1)}, f32[2048,128]{0,1:T(8,128)S(1)}) fusion(f32[2048,128]{0,1:T(8,128)} %fusion.50, bf16[2048,64]{1,0:T(8,128)(2,1)S(1)} %bitcast.98, bf16[128,64]{0,1:T(8,128)(2,1)S(1)} %copy-done.7, s32[128]{0:T(128)S(1)} %broadcast_select_fusion.6, s32[128]{0:T(128)S(1)} %broadcast_select_fusion.7, pred[2048]{0:T(1024)(128)(4,1)S(1)} %fusion.29), kind=kOutput, calls=%fused_computation.114 | convolution fusion | flops 35125248 | bytes 2386944 | tf_op jit(solution)/shard_map/rd,kd->rk/dot_general | solution.py:58
  27.8 1.3 %broadcast_select_fusion.2 = s32[128]{0:T(128)S(1)} fusion(s32[]{:T(128)} %bitcast.13, s32[]{:T(128)} %bitcast.12), kind=kLoop, calls=%fused_computation.98 | loop fusion | flops 1280 | bytes 520 | tf_op jit(solution)/shard_map/jit(_where)/select_n | solution.py:28
  29.6 5.5 %collective-permute-done.3 = bf16[128,64]{0,1:T(8,128)(2,1)S(1)} collective-permute-done((bf16[128,64]{0,1:T(8,128)(2,1)S(1)}, bf16[128,64]{0,1:T(8,128)(2,1)S(1)}, u32[]{:S(2)}, u32[]{:S(2)}) %collective-permute-start.3) | collective-permute-done | bytes 16416 | tf_op jit(solution)/shard_map/ppermute | solution.py:15
  35.4 5.5 %collective-permute-done.5 = bf16[128,64]{0,1:T(8,128)(2,1)S(1)} collective-permute-done((bf16[128,64]{0,1:T(8,128)(2,1)S(1)}, bf16[128,64]{0,1:T(8,128)(2,1)S(1)}, u32[]{:S(2)}, u32[]{:S(2)}) %collective-permute-start.5) | collective-permute-done | bytes 16416 | tf_op jit(solution)/shard_map/ppermute | solution.py:15
  42.3 6.2 %collective-permute-done.2 = bf16[128,512]{1,0:T(8,128)(2,1)S(1)} collective-permute-done((bf16[128,512]{1,0:T(8,128)(2,1)S(1)}, bf16[128,512]{1,0:T(8,128)(2,1)S(1)}, u32[]{:S(2)}, u32[]{:S(2)}) %collective-permute-start.2) | collective-permute-done | bytes 131104 | tf_op jit(solution)/shard_map/ppermute | solution.py:15
  49.3 6.2 %collective-permute-done.4 = bf16[128,512]{1,0:T(8,128)(2,1)S(1)} collective-permute-done((bf16[128,512]{1,0:T(8,128)(2,1)S(1)}, bf16[128,512]{1,0:T(8,128)(2,1)S(1)}, u32[]{:S(2)}, u32[]{:S(2)}) %collective-permute-start.4) | collective-permute-done | bytes 131104 | tf_op jit(solution)/shard_map/ppermute | solution.py:15
  59.9 1.1 multiply_convert_fusion.1
  66.8 2.3 %multiply_convert_fusion = bf16[2048,512]{1,0:T(8,128)(2,1)} fusion(f32[2048,512]{1,0:T(8,128)S(1)} %fusion.56, f32[2048,512]{1,0:T(8,128)S(1)} %fusion.54, f32[2048,512]{1,0:T(8,128)S(1)} %fusion.55, bf16[2048,128]{0,1:T(8,128)(2,1)S(1)} %get-tuple-element.29, bf16[128,512]{1,0:T(8,128)(2,1)S(1)} %collective-permute-done.4), kind=kOutput, calls=%fused_computation | convolution fusion | flops 273678336 | bytes 15335424 | tf_op jit(solution)/shard_map/dot_general | solution.py:82
  69.9 3.8 %collective-permute-done.6 = f32[128,512]{1,0:T(8,128)S(1)} collective-permute-done((f32[128,512]{1,0:T(8,128)S(1)}, f32[128,512]{1,0:T(8,128)S(1)}, u32[]{:S(2)}, u32[]{:S(2)}) %collective-permute-start.6) | collective-permute-done | bytes 262176 | tf_op jit(solution)/shard_map/ppermute | solution.py:15
  74.7 1.3 %collective-permute-done.11 = f32[128,64]{0,1:T(8,128)S(1)} collective-permute-done((f32[128,64]{0,1:T(8,128)S(1)}, f32[128,64]{0,1:T(8,128)S(1)}, u32[]{:S(2)}, u32[]{:S(2)}) %collective-permute-start.11) | collective-permute-done | bytes 32800 | tf_op jit(solution)/shard_map/ppermute | solution.py:15
  76.3 6.6 %collective-permute-done.7 = f32[128,512]{1,0:T(8,128)S(1)} collective-permute-done((f32[128,512]{1,0:T(8,128)S(1)}, f32[128,512]{1,0:T(8,128)S(1)}, u32[]{:S(2)}, u32[]{:S(2)}) %collective-permute-start.7) | collective-permute-done | bytes 262176 | tf_op jit(solution)/shard_map/ppermute | solution.py:15
  83.7 1.0 fusion.57
  84.8 2.1 %collective-permute-done.13 = bf16[128,64]{0,1:T(8,128)(2,1)S(1)} collective-permute-done((bf16[128,64]{0,1:T(8,128)(2,1)S(1)}, bf16[128,64]{0,1:T(8,128)(2,1)S(1)}, u32[]{:S(2)}, u32[]{:S(2)}) %collective-permute-start.13) | collective-permute-done | bytes 16416 | tf_op jit(solution)/shard_map/ppermute | solution.py:15
  87.7 5.0 %collective-permute-done.8 = f32[128,512]{1,0:T(8,128)} collective-permute-done((f32[128,512]{1,0:T(8,128)}, f32[128,512]{1,0:T(8,128)}, u32[]{:S(2)}, u32[]{:S(2)}) %collective-permute-start.8) | collective-permute-done | bytes 262176 | tf_op jit(solution)/shard_map/ppermute | solution.py:15
  92.7 1.0 add_convert_fusion
  93.7 2.2 %convolution_add_fusion.6 = f32[2048,64]{0,1:T(8,128)} fusion(f32[2048,64]{0,1:T(8,128)} %fusion.57, bf16[128,64]{0,1:T(8,128)(2,1)} %copy-done.8, bf16[2048,128]{0,1:T(8,128)(2,1)} %copy-done.2), kind=kOutput, calls=%fused_computation.16 | convolution fusion | flops 33685504 | bytes 1589248 | tf_op jit(solution)/shard_map/dot_general | solution.py:85
  96.0 2.1 %collective-permute-done.9 = bf16[128,512]{1,0:T(8,128)(2,1)S(1)} collective-permute-done((bf16[128,512]{1,0:T(8,128)(2,1)S(1)}, bf16[128,512]{1,0:T(8,128)(2,1)S(1)}, u32[]{:S(2)}, u32[]{:S(2)}) %collective-permute-start.9) | collective-permute-done | bytes 131104 | tf_op jit(solution)/shard_map/ppermute | solution.py:15
  98.8 1.3 %convolution_add_fusion.5 = f32[2048,64]{0,1:T(8,128)S(1)} fusion(f32[2048,64]{0,1:T(8,128)} %convolution_add_fusion.6, bf16[128,64]{0,1:T(8,128)(2,1)} %copy-done.9, bf16[2048,128]{0,1:T(8,128)(2,1)S(1)} %get-tuple-element.31), kind=kOutput, calls=%fused_computation.15 | convolution fusion | flops 33685504 | bytes 1589248 | tf_op jit(solution)/shard_map/dot_general | solution.py:85
  100.6 1.1 copy.18
  103.3 10.4 %reduce-scatter.5.cloned.1.call-done = bf16[64,512]{1,0:T(8,128)(2,1)} async-done(((bf16[128,512]{1,0:T(8,128)(2,1)}), bf16[64,512]{1,0:T(8,128)(2,1)}) %reduce-scatter.5.cloned.1.call-update) | async-done | bytes 65552 | tf_op jit(solution)/shard_map/reduce_scatter | solution.py:108
  113.6 1.5 %convert_element_type.57 = f32[64,512]{1,0:T(8,128)} convert(bf16[64,512]{1,0:T(8,128)(2,1)} %reduce-scatter.5.cloned.1.call-done) | non-fusion elementwise | flops 32768 | bytes 196608 | tf_op jit(solution)/shard_map/convert_element_type | solution.py:107
  (84 shorter events, 21.2 us)
Async XLA Ops:
  7.2 49.3 %copy-start = (bf16[128,16,512]{2,1,0:T(8,128)(2,1)S(1)}, bf16[128,16,512]{2,1,0:T(8,128)(2,1)}, u32[]{:S(2)}) copy-start(bf16[128,16,512]{2,1,0:T(8,128)(2,1)} %param.10) | copy-start | bytes 6291460
  7.2 94.5 %reduce-scatter.7.cloned.1.call-start = ((), (), s32[]{:S(2)}) async-start(), calls=%async_computation.3 | async-start | bytes 49152
  7.2 21.9 %collective-permute-start.1 = (bf16[128,64]{0,1:T(8,128)(2,1)}, bf16[128,64]{0,1:T(8,128)(2,1)S(1)}, u32[]{:S(2)}, u32[]{:S(2)}) collective-permute-start(bf16[128,64]{0,1:T(8,128)(2,1)} %param.9), channel_id=1, source_target_pairs={{30,0},{0,2},{2,4},{4,6},{6,8},{8,10},{10,12},{12,14},{14,16},{16,... | collective-permute-start | bytes 49160 | tf_op jit(solution)/shard_map/ppermute | solution.py:15
  7.7 33.5 %collective-permute-start = (bf16[128,512]{1,0:T(8,128)(2,1)}, bf16[128,512]{1,0:T(8,128)(2,1)S(1)}, u32[]{:S(2)}, u32[]{:S(2)}) collective-permute-start(bf16[128,512]{1,0:T(8,128)(2,1)} %param.8), channel_id=1, source_target_pairs={{30,0},{0,2},{2,4},{4,6},{6,8},{8,10},{10,12},{12,14},{14,16},{16,... | collective-permute-start | bytes 393224 | tf_op jit(solution)/shard_map/ppermute | solution.py:15
  10.4 15.8 %copy-start.7 = (bf16[128,64]{0,1:T(8,128)(2,1)S(1)}, bf16[128,64]{0,1:T(8,128)(2,1)}, u32[]{:S(2)}) copy-start(bf16[128,64]{0,1:T(8,128)(2,1)} %param.9) | copy-start | bytes 49156
  29.1 12.2 %copy-start.1 = (bf16[128,16,512]{2,1,0:T(8,128)(2,1)S(1)}, bf16[128,16,512]{2,1,0:T(8,128)(2,1)}, u32[]{:S(2)}) copy-start(bf16[128,16,512]{2,1,0:T(8,128)(2,1)} %param.6) | copy-start | bytes 6291460
  29.1 12.1 %copy-start.8 = (bf16[128,64]{0,1:T(8,128)(2,1)}, bf16[128,64]{0,1:T(8,128)(2,1)S(1)}, u32[]{:S(2)}) copy-start(bf16[128,64]{0,1:T(8,128)(2,1)S(1)} %collective-permute-done.1) | copy-start | bytes 49156
  29.1 5.9 %collective-permute-start.3 = (bf16[128,64]{0,1:T(8,128)(2,1)S(1)}, bf16[128,64]{0,1:T(8,128)(2,1)S(1)}, u32[]{:S(2)}, u32[]{:S(2)}) collective-permute-start(bf16[128,64]{0,1:T(8,128)(2,1)S(1)} %collective-permute-done.1), channel_id=1, source_target_pairs={{30,0},{0,2},{2,4},{4,6},{6,8},{8,10},{10,12},{12,14},{14,16},{16,... | collective-permute-start | bytes 49160 | tf_op jit(solution)/shard_map/ppermute | solution.py:15
  35.1 7.2 %copy-start.9 = (bf16[128,64]{0,1:T(8,128)(2,1)}, bf16[128,64]{0,1:T(8,128)(2,1)S(1)}, u32[]{:S(2)}) copy-start(bf16[128,64]{0,1:T(8,128)(2,1)S(1)} %collective-permute-done.3) | copy-start | bytes 49156
  35.1 5.9 %collective-permute-start.5 = (bf16[128,64]{0,1:T(8,128)(2,1)S(1)}, bf16[128,64]{0,1:T(8,128)(2,1)S(1)}, u32[]{:S(2)}, u32[]{:S(2)}) collective-permute-start(bf16[128,64]{0,1:T(8,128)(2,1)S(1)} %collective-permute-done.3), channel_id=1, source_target_pairs={{30,0},{0,2},{2,4},{4,6},{6,8},{8,10},{10,12},{12,14},{14,16},{16,... | collective-permute-start | bytes 49160 | tf_op jit(solution)/shard_map/ppermute | solution.py:15
  40.9 1.3 %copy-start.10 = (bf16[128,64]{0,1:T(8,128)(2,1)}, bf16[128,64]{0,1:T(8,128)(2,1)S(1)}, u32[]{:S(2)}) copy-start(bf16[128,64]{0,1:T(8,128)(2,1)S(1)} %collective-permute-done.5) | copy-start | bytes 49156
  41.3 7.1 %collective-permute-start.2 = (bf16[128,512]{1,0:T(8,128)(2,1)S(1)}, bf16[128,512]{1,0:T(8,128)(2,1)S(1)}, u32[]{:S(2)}, u32[]{:S(2)}) collective-permute-start(bf16[128,512]{1,0:T(8,128)(2,1)S(1)} %collective-permute-done), channel_id=1, source_target_pairs={{30,0},{0,2},{2,4},{4,6},{6,8},{8,10},{10,12},{12,14},{14,16},{16,... | collective-permute-start | bytes 393224 | tf_op jit(solution)/shard_map/ppermute | solution.py:15
  48.4 7.1 %collective-permute-start.4 = (bf16[128,512]{1,0:T(8,128)(2,1)S(1)}, bf16[128,512]{1,0:T(8,128)(2,1)S(1)}, u32[]{:S(2)}, u32[]{:S(2)}) collective-permute-start(bf16[128,512]{1,0:T(8,128)(2,1)S(1)} %collective-permute-done.2), channel_id=1, source_target_pairs={{30,0},{0,2},{2,4},{4,6},{6,8},{8,10},{10,12},{12,14},{14,16},{16,... | collective-permute-start | bytes 393224 | tf_op jit(solution)/shard_map/ppermute | solution.py:15
  49.3 7.1 %copy-start.5 = (bf16[128,512]{1,0:T(8,128)(2,1)S(1)}, bf16[128,512]{1,0:T(8,128)(2,1)}, u32[]{:S(2)}) copy-start(bf16[128,512]{1,0:T(8,128)(2,1)} %param.8) | copy-start | bytes 393220
  61.0 8.5 %copy-start.2 = (bf16[2048,128]{0,1:T(8,128)(2,1)}, bf16[2048,128]{0,1:T(8,128)(2,1)S(1)}, u32[]{:S(2)}) copy-start(bf16[2048,128]{0,1:T(8,128)(2,1)S(1)} %get-tuple-element.30) | copy-start | bytes 1572868
  61.0 15.0 %copy-start.3 = (bf16[2048,128]{0,1:T(8,128)(2,1)}, bf16[2048,128]{0,1:T(8,128)(2,1)S(1)}, u32[]{:S(2)}) copy-start(bf16[2048,128]{0,1:T(8,128)(2,1)S(1)} %get-tuple-element.29) | copy-start | bytes 1572868
  62.5 7.0 %collective-permute-start.10 = (f32[128,64]{0,1:T(8,128)S(1)}, f32[128,64]{0,1:T(8,128)S(1)}, u32[]{:S(2)}, u32[]{:S(2)}) collective-permute-start(f32[128,64]{0,1:T(8,128)S(1)} %convolution_multiply_fusion.7), channel_id=1, source_target_pairs={{30,0},{0,2},{2,4},{4,6},{6,8},{8,10},{10,12},{12,14},{14,16},{16,... | collective-permute-start | bytes 98312 | tf_op jit(solution)/shard_map/ppermute | solution.py:15
  65.0 8.7 %collective-permute-start.6 = (f32[128,512]{1,0:T(8,128)S(1)}, f32[128,512]{1,0:T(8,128)S(1)}, u32[]{:S(2)}, u32[]{:S(2)}) collective-permute-start(f32[128,512]{1,0:T(8,128)S(1)} %convolution_add_fusion.10), channel_id=1, source_target_pairs={{30,0},{0,2},{2,4},{4,6},{6,8},{8,10},{10,12},{12,14},{14,16},{16,... | collective-permute-start | bytes 786440 | tf_op jit(solution)/shard_map/ppermute | solution.py:15
  69.9 6.1 %collective-permute-start.11 = (f32[128,64]{0,1:T(8,128)S(1)}, f32[128,64]{0,1:T(8,128)S(1)}, u32[]{:S(2)}, u32[]{:S(2)}) collective-permute-start(f32[128,64]{0,1:T(8,128)S(1)} %fusion.11), channel_id=1, source_target_pairs={{30,0},{0,2},{2,4},{4,6},{6,8},{8,10},{10,12},{12,14},{14,16},{16,... | collective-permute-start | bytes 98312 | tf_op jit(solution)/shard_map/ppermute | solution.py:15
  74.2 8.6 %collective-permute-start.7 = (f32[128,512]{1,0:T(8,128)S(1)}, f32[128,512]{1,0:T(8,128)S(1)}, u32[]{:S(2)}, u32[]{:S(2)}) collective-permute-start(f32[128,512]{1,0:T(8,128)S(1)} %fusion.10), channel_id=1, source_target_pairs={{30,0},{0,2},{2,4},{4,6},{6,8},{8,10},{10,12},{12,14},{14,16},{16,... | collective-permute-start | bytes 786440 | tf_op jit(solution)/shard_map/ppermute | solution.py:15
  76.0 7.7 %collective-permute-start.12 = (f32[128,64]{0,1:T(8,128)S(1)}, f32[128,64]{0,1:T(8,128)S(1)}, u32[]{:S(2)}, u32[]{:S(2)}) collective-permute-start(f32[128,64]{0,1:T(8,128)S(1)} %add.248), channel_id=1, source_target_pairs={{30,0},{0,2},{2,4},{4,6},{6,8},{8,10},{10,12},{12,14},{14,16},{16,... | collective-permute-start | bytes 98312 | tf_op jit(solution)/shard_map/ppermute | solution.py:15
  83.6 9.0 %collective-permute-start.8 = (f32[128,512]{1,0:T(8,128)}, f32[128,512]{1,0:T(8,128)}, u32[]{:S(2)}, u32[]{:S(2)}) collective-permute-start(f32[128,512]{1,0:T(8,128)} %add.244), channel_id=1, source_target_pairs={{30,0},{0,2},{2,4},{4,6},{6,8},{8,10},{10,12},{12,14},{14,16},{16,... | collective-permute-start | bytes 786440 | tf_op jit(solution)/shard_map/ppermute | solution.py:15
  83.7 3.2 %collective-permute-start.13 = (bf16[128,64]{0,1:T(8,128)(2,1)S(1)}, bf16[128,64]{0,1:T(8,128)(2,1)S(1)}, u32[]{:S(2)}, u32[]{:S(2)}) collective-permute-start(bf16[128,64]{0,1:T(8,128)(2,1)S(1)} %add_convert_fusion.1), channel_id=1, source_target_pairs={{6,0},{8,2},{10,4},{12,6},{14,8},{16,10},{18,12},{20,14},{22,16},{... | collective-permute-start | bytes 49160 | tf_op jit(solution)/shard_map/ppermute | solution.py:15
  84.7 15.3 %copy-start.4 = (bf16[2048,128]{0,1:T(8,128)(2,1)S(1)}, bf16[2048,128]{0,1:T(8,128)(2,1)}, u32[]{:S(2)}) copy-start(bf16[2048,128]{0,1:T(8,128)(2,1)} %copy-done.3) | copy-start | bytes 1572868
  84.8 15.3 %copy-start.11 = (bf16[128,64]{0,1:T(8,128)(2,1)S(1)}, bf16[128,64]{0,1:T(8,128)(2,1)}, u32[]{:S(2)}) copy-start(bf16[128,64]{0,1:T(8,128)(2,1)} %copy-done.10) | copy-start | bytes 49156
  87.6 26.0 %reduce-scatter.5.cloned.1.call-start = ((), (), s32[]{:S(2)}) async-start(), calls=%async_computation.2 | async-start | bytes 196608 | tf_op jit(solution)/shard_map/reduce_scatter | solution.py:108
  93.6 4.4 %collective-permute-start.9 = (bf16[128,512]{1,0:T(8,128)(2,1)S(1)}, bf16[128,512]{1,0:T(8,128)(2,1)S(1)}, u32[]{:S(2)}, u32[]{:S(2)}) collective-permute-start(bf16[128,512]{1,0:T(8,128)(2,1)S(1)} %add_convert_fusion), channel_id=1, source_target_pairs={{6,0},{8,2},{10,4},{12,6},{14,8},{16,10},{18,12},{20,14},{22,16},{... | collective-permute-start | bytes 393224 | tf_op jit(solution)/shard_map/ppermute | solution.py:15
  98.1 0.7 copy-start.6
Sparse Core Ops, SparseCore 0:
  87.7 12.7 reduce-scatter.6
  103.3 10.2 reduce-scatter.4
where the time goes:
time: 123 us; the launch traced here: 122 us
  waiting for transfers between devices  54.7 us (44%)
  matrix products  26.5 us (22%)
  other arithmetic  14.5 us (12%)
  between operations  14.5 us (12%)
  local copies, waits for them, and re-layouts  7.86 us (6%)
  starting transfers between devices  3.91 us (3%)
    ppermute x14, waiting for transfers between devices, from_behind(): return lax.ppermute(block, axis, route)  44.3 us
    reduce_scatter x1, waiting for transfers between devices, on_device(): lax.psum_scatter(for_sending(homed), 'hg', scatter_dimension=0, tiled=True)  10.4 us
    dot_general x4, matrix products, on_device(): jnp.einsum('rd,kd->rk', query_plain, current[0], preferred_element_type=j...  5.99 us
    unnamed x29, local copies, waits for them, and re-layouts  5.47 us
    select_n x4, other arithmetic, allowed_tile(): lower = jnp.where(key_half == 0, tile[1, 0], tile[1, 1])  5.1 us
    select_n x4, other arithmetic, allowed_tile(): upper = jnp.where(key_half == 0, tile[0, 0], tile[0, 1])  5.02 us
    dot_general x4, matrix products, on_device(): jnp.dot(dscore, k_rope, preferred_element_type=jnp.float32)  4.78 us
    dot_general x4, matrix products, on_device(): jnp.dot(dscore, k_nope, preferred_element_type=jnp.float32)  4.49 us
  transfers between devices with their start and end apart: 16, of which 11 were waited for; matrix products, arithmetic and copies ran while one was open for 33% of the time, Pallas kernels for 0%

commit v1 on v0

v1 whole, which is shorter than its diff:
```python
import functools
import math

import jax
import jax.numpy as jnp
from jax import lax
from jax.experimental import pallas as pl
from jax.experimental.pallas import tpu as pltpu
from jax.sharding import PartitionSpec as P

WINDOW = 4
PAIRS = WINDOW // 2
SCORE_SCALE = 192.0 ** (-0.5)
LOG2E = math.log2(math.e)
LANES = 128
MESH = pl.DeviceIdType.MESH


def dot_nt(a, b):
    return lax.dot_general(a, b, (((1,), (1,)), ((), ())), preferred_element_type=jnp.float32)


def dot_tn(a, b):
    return lax.dot_general(a, b, (((0,), (0,)), ((), ())), preferred_element_type=jnp.float32)


def kernel(
    n_ctx,
    n_hg,
    mask_ref,
    q_hbm,
    qr_hbm,
    kn_hbm,
    kr_hbm,
    g_hbm,
    dq_ref,
    dqr_ref,
    dkn_ref,
    dkr_ref,
    q_ref,
    qr_ref,
    g_ref,
    kr_own,
    kcat,
    x_ref,
    dp_ref,
    prob_ref,
    ds_ref,
    bias_ref,
    acc_ref,
    dk_out,
    dk_in,
    load_sem,
    k_send,
    k_recv,
    d_send,
    d_recv,
):
    rows, latent = q_ref.shape
    rope = qr_ref.shape[1]
    keys = kcat.shape[1]
    piece = keys // n_hg
    pair = 2 * keys
    blocks = mask_ref.shape[0] // n_ctx
    block_rows = rows // blocks
    tile = 256
    tiles = rows // tile
    c = lax.axis_index("ctx")
    h = lax.axis_index("hg")

    load_kn = pltpu.make_async_copy(kn_hbm, kcat.at[0, :, pl.ds(0, latent)], load_sem.at[0])
    load_kr = pltpu.make_async_copy(kr_hbm, kr_own, load_sem.at[1])
    load_q = pltpu.make_async_copy(q_hbm, q_ref, load_sem.at[2])
    load_qr = pltpu.make_async_copy(qr_hbm, qr_ref, load_sem.at[3])
    load_g = pltpu.make_async_copy(g_hbm, g_ref, load_sem.at[4])
    load_kn.start()
    load_kr.start()

    barrier = pltpu.get_barrier_semaphore()
    greeted = 0
    for d in range(1 - WINDOW, WINDOW):
        for k in range(n_hg):
            if d == 0 and k == 0:
                continue
            pl.semaphore_signal(
                barrier,
                inc=1,
                device_id=(lax.rem(c + d + n_ctx, n_ctx), lax.rem(h + k, n_hg)),
                device_id_type=MESH,
            )
            greeted += 1
    load_q.start()
    load_qr.start()
    load_g.start()

    load_kn.wait()
    load_kr.wait()
    kcat[0, :, latent:] = jnp.zeros((keys, kcat.shape[2] - latent), kcat.dtype)
    kcat[0, :, latent : latent + rope] = kr_own[...]
    pl.semaphore_wait(barrier, greeted)

    sends = []
    for d in range(1, WINDOW):
        copy = pltpu.make_async_remote_copy(
            src_ref=kcat.at[0],
            dst_ref=kcat.at[d],
            send_sem=k_send.at[d],
            recv_sem=k_recv.at[d],
            device_id=(lax.rem(c + d, n_ctx), h),
            device_id_type=MESH,
        )
        copy.start()
        sends.append(copy)

    key_block = lax.broadcasted_iota(jnp.int32, (1, WINDOW * keys), 1) // (keys // blocks)
    for rb in range(blocks):
        bias = jnp.zeros((1, WINDOW * keys), jnp.float32)
        for d in range(WINDOW):
            source = lax.rem(c - d + n_ctx, n_ctx)
            for kb in range(blocks):
                bit = mask_ref[c * blocks + rb, source * blocks + kb]
                value = jnp.where(bit == 1, 0.0, -jnp.inf).astype(jnp.float32)
                bias = jnp.where(key_block == d * blocks + kb, value, bias)
        bias_ref[rb : rb + 1, :] = bias

    acc_ref[...] = jnp.zeros_like(acc_ref)
    load_q.wait()
    load_qr.wait()
    load_g.wait()

    for p in range(PAIRS):
        for d in (2 * p, 2 * p + 1):
            if d > 0:
                sends[d - 1].wait_recv()
        cols = slice(p * pair, (p + 1) * pair)

        def score_tile(i, _, p=p, cols=cols):
            r = pl.ds(pl.multiple_of(i * tile, tile), tile)
            kn = kcat[2 * p : 2 * p + 2, :, :latent].reshape(pair, latent)
            kr = kcat[2 * p : 2 * p + 2, :, latent : latent + rope].reshape(pair, rope)
            bias = bias_ref[pl.ds(i * tile // block_rows, 1), cols]
            s = dot_nt(q_ref[r, :], kn) + dot_nt(qr_ref[r, :], kr)
            x_ref[r, cols] = s * (SCORE_SCALE * LOG2E) + bias
            dp_ref[r, cols] = dot_nt(g_ref[r, :], kn)
            return 0

        lax.fori_loop(0, tiles, score_tile, 0)

    def add_key_grads(p, r, ds, prob):
        q = q_ref[r, :]
        acc_ref[p, :, :latent] += dot_tn(ds, q) + dot_tn(prob, g_ref[r, :])
        acc_ref[p, :, latent : latent + rope] += dot_tn(ds, qr_ref[r, :])

    def send_key_grads(p):
        out = []
        for d in (2 * p + 1, 2 * p):
            block = acc_ref[p, (d - 2 * p) * keys : (d - 2 * p + 1) * keys, :]
            dk_out[d] = block.reshape(n_hg, piece, block.shape[1]).astype(dk_out.dtype)
            for k in reversed(range(n_hg)):
                if d == 0 and k == 0:
                    continue
                peer = lax.rem(h + k, n_hg)
                copy = pltpu.make_async_remote_copy(
                    src_ref=dk_out.at[d, peer],
                    dst_ref=dk_in.at[d, k],
                    send_sem=d_send.at[d, k],
                    recv_sem=d_recv.at[d, k],
                    device_id=(lax.rem(c - d + n_ctx, n_ctx), peer),
                    device_id_type=MESH,
                )
                copy.start()
                out.append((d, k, copy))
        return out

    last = PAIRS - 1

    def soft_tile(i, _):
        r = pl.ds(pl.multiple_of(i * tile, tile), tile)
        x = x_ref[r, :]
        dp = dp_ref[r, :]
        e = jnp.exp2(x - jnp.max(x, axis=1, keepdims=True))
        inv = 1.0 / jnp.sum(e, axis=1, keepdims=True)
        delta = jnp.sum(e * dp, axis=1, keepdims=True) * inv
        prob = (e * inv).astype(jnp.bfloat16)
        ds = (e * (inv * SCORE_SCALE) * (dp - delta)).astype(jnp.bfloat16)
        prob_ref[r, :] = prob
        ds_ref[r, :] = ds
        add_key_grads(last, r, ds[:, last * pair :], prob[:, last * pair :])
        return 0

    lax.fori_loop(0, tiles, soft_tile, 0)
    moving = send_key_grads(last)

    for p in reversed(range(last)):
        cols = slice(p * pair, (p + 1) * pair)

        def grad_tile(i, _, p=p, cols=cols):
            r = pl.ds(pl.multiple_of(i * tile, tile), tile)
            add_key_grads(p, r, ds_ref[r, cols], prob_ref[r, cols])
            return 0

        lax.fori_loop(0, tiles, grad_tile, 0)
        moving += send_key_grads(p)

    def query_tile(i, _):
        r = pl.ds(pl.multiple_of(i * tile, tile), tile)
        ds = ds_ref[r, :]
        kn = kcat[:, :, :latent].reshape(WINDOW * keys, latent)
        kr = kcat[:, :, latent : latent + rope].reshape(WINDOW * keys, rope)
        dq_ref[r, :] = jnp.dot(ds, kn, preferred_element_type=jnp.float32).astype(dq_ref.dtype)
        dqr_ref[r, :] = jnp.dot(ds, kr, preferred_element_type=jnp.float32).astype(dqr_ref.dtype)
        return 0

    lax.fori_loop(0, tiles, query_tile, 0)

    total = acc_ref[0, pl.ds(pl.multiple_of(h * piece, piece), piece), :]
    for d, k, copy in sorted(moving, key=lambda m: (-m[0], m[1])):
        copy.wait_recv()
        total = total + dk_in[d, k].astype(jnp.float32)
    dkn_ref[...] = total[:, :latent]
    dkr_ref[...] = total[:, latent : latent + rope]

    for copy in sends:
        copy.wait_send()
    for _, _, copy in moving:
        copy.wait_send()


def on_device(n_ctx, n_hg, q, qr, kn, kr, g, block_mask):
    tokens, heads, latent = q.shape
    rope = qr.shape[2]
    rows = tokens * heads
    width = -(-(latent + rope) // LANES) * LANES
    piece = tokens // n_hg
    blocks = block_mask.shape[0] // n_ctx
    bf16, f32 = jnp.bfloat16, jnp.float32
    hbm = pl.BlockSpec(memory_space=pl.ANY)
    vmem = pl.BlockSpec(memory_space=pltpu.VMEM)
    dq, dqr, dkn, dkr = pl.pallas_call(
        functools.partial(kernel, n_ctx, n_hg),
        out_shape=(
            jax.ShapeDtypeStruct((rows, latent), bf16),
            jax.ShapeDtypeStruct((rows, rope), bf16),
            jax.ShapeDtypeStruct((piece, latent), f32),
            jax.ShapeDtypeStruct((piece, rope), f32),
        ),
        in_specs=[pl.BlockSpec(memory_space=pltpu.SMEM)] + [hbm] * 5,
        out_specs=[vmem] * 4,
        scratch_shapes=[
            pltpu.VMEM((rows, latent), bf16),
            pltpu.VMEM((rows, rope), bf16),
            pltpu.VMEM((rows, latent), bf16),
            pltpu.VMEM((tokens, rope), bf16),
            pltpu.VMEM((WINDOW, tokens, width), bf16),
            pltpu.VMEM((rows, WINDOW * tokens), f32),
            pltpu.VMEM((rows, WINDOW * tokens), f32),
            pltpu.VMEM((rows, WINDOW * tokens), bf16),
            pltpu.VMEM((rows, WINDOW * tokens), bf16),
            pltpu.VMEM((blocks, WINDOW * tokens), f32),
            pltpu.VMEM((PAIRS, 2 * tokens, width), f32),
            pltpu.VMEM((WINDOW, n_hg, piece, width), bf16),
            pltpu.VMEM((WINDOW, n_hg, piece, width), bf16),
            pltpu.SemaphoreType.DMA((5,)),
            pltpu.SemaphoreType.DMA((WINDOW,)),
            pltpu.SemaphoreType.DMA((WINDOW,)),
            pltpu.SemaphoreType.DMA((WINDOW, n_hg)),
            pltpu.SemaphoreType.DMA((WINDOW, n_hg)),
        ],
        compiler_params=pltpu.CompilerParams(
            collective_id=0, has_side_effects=True, vmem_limit_bytes=44 * 1024 * 1024
        ),
    )(block_mask, q.reshape(rows, latent), qr.reshape(rows, rope), kn, kr, g.reshape(rows, latent))
    return dq.reshape(tokens, heads, latent), dqr.reshape(tokens, heads, rope), dkn, dkr


def solution(mesh):
    wide = P("ctx", "hg", None)
    owned = P(("ctx", "hg"), None)
    return jax.shard_map(
        functools.partial(on_device, mesh.shape["ctx"], mesh.shape["hg"]),
        mesh=mesh,
        in_specs=(wide, wide, P("ctx", None), P("ctx", None), wide, P()),
        out_specs=(wide, wide, owned, owned),
        check_vma=False,
    )
```

time: 123 us -> 45.1 us (0.37)
  waiting for transfers between devices: 54.7 us -> 0 us
  Pallas kernels: 0 us -> 33.2 us
  matrix products: 26.5 us -> 0 us
  other arithmetic: 14.5 us -> 0 us
  between operations: 14.5 us -> 0.66 us
  starting transfers between devices: 3.91 us -> 0 us
  local copies, waits for them, and re-layouts: 7.86 us -> 10.7 us
    ppermute x14 -> x0, waiting for transfers between devices: 44.3 us -> none  [from_behind(): return lax.ppermute(block, axis, route)]
    pallas_call x0 -> x1, Pallas kernels: none -> 33.2 us  [on_device(): pl.pallas_call(functools.partial(kernel, n_ctx, n_hg), out_shape=(jax.Sha...]
    dot_general x32 -> x0, matrix products: 26.5 us -> none  [the longest x4 5.99 us: on_device(): jnp.einsum('rd,kd->rk', query_plain, current[0], preferred_element_type=j...]
    reduce_scatter x1 -> x0, waiting for transfers between devices: 10.4 us -> none  [on_device(): lax.psum_scatter(for_sending(homed), 'hg', scatter_dimension=0, tiled=True)]
    select_n x8 -> x0, other arithmetic: 10.1 us -> none  [the longest x4 5.1 us: allowed_tile(): lower = jnp.where(key_half == 0, tile[1, 0], tile[1, 1])]
    unnamed x29 -> x14, local copies, waits for them, and re-layouts: 5.47 us -> 10.7 us
    ppermute x14 -> x0, starting transfers between devices: 3.84 us -> none  [from_behind(): return lax.ppermute(block, axis, route)]
    convert_element_type x4 -> x0, other arithmetic: 3.57 us -> none  [the longest x1 1.5 us: on_device(): part.astype(jnp.float32)]
  transfers between devices with their start and end apart: 16 -> 0, of which waited for: 11 -> 0; matrix products, arithmetic and copies ran while one was open for 33% -> 0% of each run, Pallas kernels for 0% -> 0%
where the time goes in v1:
time: 45.1 us; the launch traced here: 44.6 us
  Pallas kernels  33.2 us (74%)
  local copies, waits for them, and re-layouts  10.7 us (24%)
  between operations  0.66 us (1%)
    pallas_call x1, Pallas kernels, on_device(): pl.pallas_call(functools.partial(kernel, n_ctx, n_hg), out_shape=(jax.Sha...  33.2 us
    unnamed x14, local copies, waits for them, and re-layouts  10.7 us

profile of v1, /device:TPU:0, one launch (start us, length us, event | category | flops | bytes accessed | tf_op | source)
XLA Modules:
  0.0 44.6 jit_solution(7654613660090017157)
XLA Ops:
  0.6 0.8 %copy.11.kr_hbm = bf16[128,64]{1,0:T(8,128)(2,1)S(1)} copy(bf16[128,64]{0,1:T(8,128)(2,1)} %param.9) | data formatting | bytes 32768 | tf_op args[3]
  1.5 1.4 %copy.10 = bf16[128,16,64]{2,1,0:T(8,128)(2,1)S(1)} copy(bf16[128,16,64]{0,2,1:T(8,128)(2,1)} %param.7) | data formatting | bytes 524288 | tf_op args[1]
  2.8 0.0 copy-start
  2.9 1.6 %copy-done = bf16[128,16,512]{2,1,0:T(8,128)(2,1)S(1)} copy-done((bf16[128,16,512]{2,1,0:T(8,128)(2,1)S(1)}, bf16[128,16,512]{2,1,0:T(8,128)(2,1)}, u32[]{:S(2)}) %copy-start) | copy-done | bytes 2097176
  4.4 0.0 copy-start.1
  4.4 1.6 %copy-done.1 = bf16[128,16,512]{2,1,0:T(8,128)(2,1)S(1)} copy-done((bf16[128,16,512]{2,1,0:T(8,128)(2,1)S(1)}, bf16[128,16,512]{2,1,0:T(8,128)(2,1)}, u32[]{:S(2)}) %copy-start.1) | copy-done | bytes 2097176
  6.0 0.0 copy-start.2
  6.0 0.9 %copy-done.2 = bf16[128,512]{1,0:T(8,128)(2,1)S(1)} copy-done((bf16[128,512]{1,0:T(8,128)(2,1)S(1)}, bf16[128,512]{1,0:T(8,128)(2,1)}, u32[]{:S(2)}) %copy-start.2) | copy-done | bytes 131096
  6.9 0.0 copy-start.3
  6.9 0.7 %copy-done.3 = s32[32,32]{1,0:T(8,128)S(1)} copy-done((s32[32,32]{1,0:T(8,128)S(1)}, s32[32,32]{1,0:T(8,128)}, u32[]{:S(2)}) %copy-start.3) | copy-done | bytes 4120
  7.7 33.2 %shard_map.93 = (bf16[2048,512]{1,0:T(8,128)(2,1)S(1)}, bf16[2048,64]{1,0:T(8,128)(2,1)S(1)}, f32[64,512]{1,0:T(8,128)S(1)}, f32[64,64]{1,0:T(8,128)S(1)}) custom-call(s32[32,32]{1,0:T(8,128)S(1)} %copy-done.3, bf16[2048,512]{1,0:T(8,128)(2,1)S(1)} %bitcast.5, bf16[2048,64]{1,0:T(8,128)(2,1)S(1)} %bitcast.7, bf16[128,512]{1,0:T(8,128)(2,1)S(1)} %copy-done.2, ...), custom_call_target="tpu_custom_call" | custom-call | tf_op jit(solution)/shard_map/pallas_call | solution.py:239
  40.9 1.1 %copy.12 = bf16[128,16,64]{0,2,1:T(8,128)(2,1)} copy(bf16[128,16,64]{2,1,0:T(8,128)(2,1)S(1)} %bitcast.9) | data formatting | bytes 524288
  42.1 1.3 %copy.16 = bf16[128,16,512]{2,1,0:T(8,128)(2,1)} copy(bf16[128,16,512]{2,1,0:T(8,128)(2,1)S(1)} %bitcast.8) | data formatting | bytes 4194304
  43.4 0.7 %copy.17 = f32[64,512]{1,0:T(8,128)} copy(f32[64,512]{1,0:T(8,128)S(1)} %get-tuple-element.22) | data formatting | bytes 262144
  44.0 0.6 %copy.18 = f32[64,64]{1,0:T(8,128)} copy(f32[64,64]{1,0:T(8,128)S(1)} %get-tuple-element.23) | data formatting | bytes 32768
Async XLA Ops:
  2.8 1.6 %copy-start = (bf16[128,16,512]{2,1,0:T(8,128)(2,1)S(1)}, bf16[128,16,512]{2,1,0:T(8,128)(2,1)}, u32[]{:S(2)}) copy-start(bf16[128,16,512]{2,1,0:T(8,128)(2,1)} %param.6) | copy-start | bytes 6291460
  4.4 1.6 %copy-start.1 = (bf16[128,16,512]{2,1,0:T(8,128)(2,1)S(1)}, bf16[128,16,512]{2,1,0:T(8,128)(2,1)}, u32[]{:S(2)}) copy-start(bf16[128,16,512]{2,1,0:T(8,128)(2,1)} %param.10) | copy-start | bytes 6291460
  6.0 0.9 %copy-start.2 = (bf16[128,512]{1,0:T(8,128)(2,1)S(1)}, bf16[128,512]{1,0:T(8,128)(2,1)}, u32[]{:S(2)}) copy-start(bf16[128,512]{1,0:T(8,128)(2,1)} %kn_hbm.1) | copy-start | bytes 393220
  6.9 0.7 %copy-start.3 = (s32[32,32]{1,0:T(8,128)S(1)}, s32[32,32]{1,0:T(8,128)}, u32[]{:S(2)}) copy-start(s32[32,32]{1,0:T(8,128)} %mask_ref.1) | copy-start | bytes 12292

commit v2 on v1

--- a/solution.py
+++ b/solution.py
@@ -14,6 +14,10 @@
 LOG2E = math.log2(math.e)
 LANES = 128
 MESH = pl.DeviceIdType.MESH
+
+
+def dot_nn(a, b):
+    return jnp.dot(a, b, preferred_element_type=jnp.float32)
 
 
 def dot_nt(a, b):
@@ -38,10 +42,15 @@
     dkn_ref,
     dkr_ref,
     q_ref,
+    qrt_ref,
+    qr_wide,
     qr_ref,
     g_ref,
-    kr_own,
-    kcat,
+    kn_all,
+    krt_all,
+    dq_tile,
+    dqr_wide,
+    dqrt_ref,
     x_ref,
     dp_ref,
     prob_ref,
@@ -51,6 +60,7 @@
     dk_out,
     dk_in,
     load_sem,
+    store_sem,
     k_send,
     k_recv,
     d_send,
@@ -58,20 +68,24 @@
 ):
     rows, latent = q_ref.shape
     rope = qr_ref.shape[1]
-    keys = kcat.shape[1]
+    heads = qrt_ref.shape[0]
+    tokens = qrt_ref.shape[2]
+    keys = kn_all.shape[1]
     piece = keys // n_hg
     pair = 2 * keys
     blocks = mask_ref.shape[0] // n_ctx
     block_rows = rows // blocks
-    tile = 256
+    tile = 512
     tiles = rows // tile
+    soft_rows = 256
+    sub_rows = 32
     c = lax.axis_index("ctx")
     h = lax.axis_index("hg")
 
-    load_kn = pltpu.make_async_copy(kn_hbm, kcat.at[0, :, pl.ds(0, latent)], load_sem.at[0])
-    load_kr = pltpu.make_async_copy(kr_hbm, kr_own, load_sem.at[1])
+    load_kn = pltpu.make_async_copy(kn_hbm, kn_all.at[0], load_sem.at[0])
+    load_kr = pltpu.make_async_copy(kr_hbm, krt_all.at[0], load_sem.at[1])
     load_q = pltpu.make_async_copy(q_hbm, q_ref, load_sem.at[2])
-    load_qr = pltpu.make_async_copy(qr_hbm, qr_ref, load_sem.at[3])
+    load_qr = pltpu.make_async_copy(qr_hbm, qrt_ref, load_sem.at[3])
     load_g = pltpu.make_async_copy(g_hbm, g_ref, load_sem.at[4])
     load_kn.start()
     load_kr.start()
@@ -95,22 +109,23 @@
 
     load_kn.wait()
     load_kr.wait()
-    kcat[0, :, latent:] = jnp.zeros((keys, kcat.shape[2] - latent), kcat.dtype)
-    kcat[0, :, latent : latent + rope] = kr_own[...]
     pl.semaphore_wait(barrier, greeted)
 
     sends = []
     for d in range(1, WINDOW):
-        copy = pltpu.make_async_remote_copy(
-            src_ref=kcat.at[0],
-            dst_ref=kcat.at[d],
-            send_sem=k_send.at[d],
-            recv_sem=k_recv.at[d],
-            device_id=(lax.rem(c + d, n_ctx), h),
-            device_id_type=MESH,
-        )
-        copy.start()
-        sends.append(copy)
+        both = []
+        for part, buffer in enumerate((kn_all, krt_all)):
+            copy = pltpu.make_async_remote_copy(
+                src_ref=buffer.at[0],
+                dst_ref=buffer.at[d],
+                send_sem=k_send.at[d, part],
+                recv_sem=k_recv.at[d, part],
+                device_id=(lax.rem(c + d, n_ctx), h),
+                device_id_type=MESH,
+            )
+            copy.start()
+            both.append(copy)
+        sends.append(both)
 
     key_block = lax.broadcasted_iota(jnp.int32, (1, WINDOW * keys), 1) // (keys // blocks)
     for rb in range(blocks):
@@ -124,22 +139,27 @@
         bias_ref[rb : rb + 1, :] = bias
 
     acc_ref[...] = jnp.zeros_like(acc_ref)
+    load_qr.wait()
+    for head in range(heads):
+        turned = qrt_ref[head].astype(jnp.float32).T
+        qr_wide[pl.ds(head, tokens, stride=heads), :] = turned
+    qr_ref[...] = qr_wide[...].astype(qr_ref.dtype)
     load_q.wait()
-    load_qr.wait()
     load_g.wait()
 
     for p in range(PAIRS):
         for d in (2 * p, 2 * p + 1):
             if d > 0:
-                sends[d - 1].wait_recv()
+                for copy in sends[d - 1]:
+                    copy.wait_recv()
         cols = slice(p * pair, (p + 1) * pair)
 
         def score_tile(i, _, p=p, cols=cols):
             r = pl.ds(pl.multiple_of(i * tile, tile), tile)
-            kn = kcat[2 * p : 2 * p + 2, :, :latent].reshape(pair, latent)
-            kr = kcat[2 * p : 2 * p + 2, :, latent : latent + rope].reshape(pair, rope)
+            kn = kn_all[2 * p : 2 * p + 2].reshape(pair, latent)
+            krt = jnp.concatenate([krt_all[2 * p], krt_all[2 * p + 1]], axis=1)
             bias = bias_ref[pl.ds(i * tile // block_rows, 1), cols]
-            s = dot_nt(q_ref[r, :], kn) + dot_nt(qr_ref[r, :], kr)
+            s = dot_nt(q_ref[r, :], kn) + dot_nn(qr_ref[r, :], krt)
             x_ref[r, cols] = s * (SCORE_SCALE * LOG2E) + bias
             dp_ref[r, cols] = dot_nt(g_ref[r, :], kn)
             return 0
@@ -174,21 +194,19 @@
 
     last = PAIRS - 1
 
-    def soft_tile(i, _):
-        r = pl.ds(pl.multiple_of(i * tile, tile), tile)
-        x = x_ref[r, :]
-        dp = dp_ref[r, :]
-        e = jnp.exp2(x - jnp.max(x, axis=1, keepdims=True))
-        inv = 1.0 / jnp.sum(e, axis=1, keepdims=True)
-        delta = jnp.sum(e * dp, axis=1, keepdims=True) * inv
-        prob = (e * inv).astype(jnp.bfloat16)
-        ds = (e * (inv * SCORE_SCALE) * (dp - delta)).astype(jnp.bfloat16)
-        prob_ref[r, :] = prob
-        ds_ref[r, :] = ds
-        add_key_grads(last, r, ds[:, last * pair :], prob[:, last * pair :])
-        return 0
-
-    lax.fori_loop(0, tiles, soft_tile, 0)
+    for start in range(0, rows, soft_rows):
+        for at in range(start, start + soft_rows, sub_rows):
+            r = slice(at, at + sub_rows)
+            x = x_ref[r, :]
+            dp = dp_ref[r, :]
+            e = jnp.exp2(x - jnp.max(x, axis=1, keepdims=True))
+            inv = 1.0 / jnp.sum(e, axis=1, keepdims=True)
+            delta = jnp.sum(e * dp, axis=1, keepdims=True) * inv
+            prob_ref[r, :] = (e * inv).astype(jnp.bfloat16)
+            ds_ref[r, :] = (e * (inv * SCORE_SCALE) * (dp - delta)).astype(jnp.bfloat16)
+        r = slice(start, start + soft_rows)
+        cols = slice(last * pair, (last + 1) * pair)
+        add_key_grads(last, r, ds_ref[r, cols], prob_ref[r, cols])
     moving = send_key_grads(last)
 
     for p in reversed(range(last)):
@@ -202,16 +220,23 @@
         lax.fori_loop(0, tiles, grad_tile, 0)
         moving += send_key_grads(p)
 
-    def query_tile(i, _):
-        r = pl.ds(pl.multiple_of(i * tile, tile), tile)
+    stores = []
+    for i in range(tiles):
+        r = slice(i * tile, (i + 1) * tile)
         ds = ds_ref[r, :]
-        kn = kcat[:, :, :latent].reshape(WINDOW * keys, latent)
-        kr = kcat[:, :, latent : latent + rope].reshape(WINDOW * keys, rope)
-        dq_ref[r, :] = jnp.dot(ds, kn, preferred_element_type=jnp.float32).astype(dq_ref.dtype)
-        dqr_ref[r, :] = jnp.dot(ds, kr, preferred_element_type=jnp.float32).astype(dqr_ref.dtype)
-        return 0
-
-    lax.fori_loop(0, tiles, query_tile, 0)
+        kn = kn_all[...].reshape(WINDOW * keys, latent)
+        krt = jnp.concatenate([krt_all[d] for d in range(WINDOW)], axis=1)
+        dq_tile[r, :] = dot_nn(ds, kn).astype(dq_tile.dtype)
+        dqr_wide[r, :] = dot_nt(ds, krt)
+        copy = pltpu.make_async_copy(dq_tile.at[r, :], dq_ref.at[r, :], store_sem.at[i])
+        copy.start()
+        stores.append(copy)
+    for head in range(heads):
+        part = dqr_wide[pl.ds(head, tokens, stride=heads), :]
+        dqrt_ref[head] = part.T.astype(dqrt_ref.dtype)
+    copy = pltpu.make_async_copy(dqrt_ref, dqr_ref, store_sem.at[tiles])
+    copy.start()
+    stores.append(copy)
 
     total = acc_ref[0, pl.ds(pl.multiple_of(h * piece, piece), piece), :]
     for d, k, copy in sorted(moving, key=lambda m: (-m[0], m[1])):
@@ -220,8 +245,11 @@
     dkn_ref[...] = total[:, :latent]
     dkr_ref[...] = total[:, latent : latent + rope]
 
-    for copy in sends:
-        copy.wait_send()
+    for both in sends:
+        for copy in both:
+            copy.wait_send()
+    for copy in stores:
+        copy.wait()
     for _, _, copy in moving:
         copy.wait_send()
 
@@ -240,18 +268,23 @@
         functools.partial(kernel, n_ctx, n_hg),
         out_shape=(
             jax.ShapeDtypeStruct((rows, latent), bf16),
-            jax.ShapeDtypeStruct((rows, rope), bf16),
+            jax.ShapeDtypeStruct((heads, rope, tokens), bf16),
             jax.ShapeDtypeStruct((piece, latent), f32),
             jax.ShapeDtypeStruct((piece, rope), f32),
         ),
         in_specs=[pl.BlockSpec(memory_space=pltpu.SMEM)] + [hbm] * 5,
-        out_specs=[vmem] * 4,
+        out_specs=[hbm, hbm, vmem, vmem],
         scratch_shapes=[
             pltpu.VMEM((rows, latent), bf16),
+            pltpu.VMEM((heads, rope, tokens), bf16),
+            pltpu.VMEM((rows, rope), f32),
             pltpu.VMEM((rows, rope), bf16),
             pltpu.VMEM((rows, latent), bf16),
-            pltpu.VMEM((tokens, rope), bf16),
-            pltpu.VMEM((WINDOW, tokens, width), bf16),
+            pltpu.VMEM((WINDOW, tokens, latent), bf16),
+            pltpu.VMEM((WINDOW, rope, tokens), bf16),
+            pltpu.VMEM((rows, latent), bf16),
+            pltpu.VMEM((rows, rope), f32),
+            pltpu.VMEM((heads, rope, tokens), bf16),
             pltpu.VMEM((rows, WINDOW * tokens), f32),
             pltpu.VMEM((rows, WINDOW * tokens), f32),
             pltpu.VMEM((rows, WINDOW * tokens), bf16),
@@ -261,16 +294,17 @@
             pltpu.VMEM((WINDOW, n_hg, piece, width), bf16),
             pltpu.VMEM((WINDOW, n_hg, piece, width), bf16),
             pltpu.SemaphoreType.DMA((5,)),
-            pltpu.SemaphoreType.DMA((WINDOW,)),
-            pltpu.SemaphoreType.DMA((WINDOW,)),
+            pltpu.SemaphoreType.DMA((rows // 512 + 1,)),
+            pltpu.SemaphoreType.DMA((WINDOW, 2)),
+            pltpu.SemaphoreType.DMA((WINDOW, 2)),
             pltpu.SemaphoreType.DMA((WINDOW, n_hg)),
             pltpu.SemaphoreType.DMA((WINDOW, n_hg)),
         ],
         compiler_params=pltpu.CompilerParams(
-            collective_id=0, has_side_effects=True, vmem_limit_bytes=44 * 1024 * 1024
+            collective_id=0, has_side_effects=True, vmem_limit_bytes=60 * 1024 * 1024
         ),
-    )(block_mask, q.reshape(rows, latent), qr.reshape(rows, rope), kn, kr, g.reshape(rows, latent))
-    return dq.reshape(tokens, heads, latent), dqr.reshape(tokens, heads, rope), dkn, dkr
+    )(block_mask, q.reshape(rows, latent), qr.transpose(1, 2, 0), kn, kr.T, g.reshape(rows, latent))
+    return dq.reshape(tokens, heads, latent), dqr.transpose(2, 0, 1), dkn, dkr
 
 
 def solution(mesh):

time: 45.1 us -> 37 us (0.82)
  the two profiles are of different devices: /device:TPU:0 before, /device:TPU:1 now
where the time goes in v2:
time: 37 us; the launch traced here: 36.8 us
  Pallas kernels  31 us (84%)
  local copies, waits for them, and re-layouts  5.11 us (14%)
  between operations  0.67 us (2%)
    pallas_call x1, Pallas kernels, on_device(): pl.pallas_call(functools.partial(kernel, n_ctx, n_hg), out_shape=(jax.Sha...  31 us
    unnamed x10, local copies, waits for them, and re-layouts  5.11 us

profile of v2, /device:TPU:1, one launch (start us, length us, event | category | flops | bytes accessed | tf_op | source)
XLA Modules:
  0.0 36.8 jit_solution(2758749052931498056)
XLA Ops:
  0.6 31.0 %shard_map.93 = (bf16[2048,512]{1,0:T(8,128)(2,1)}, bf16[16,64,128]{2,1,0:T(8,128)(2,1)}, f32[64,512]{1,0:T(8,128)}, f32[64,64]{1,0:T(8,128)}) custom-call(s32[32,32]{1,0:T(8,128)} %mask_ref.1, bf16[2048,512]{1,0:T(8,128)(2,1)} %bitcast.6, bf16[16,64,128]{2,1,0:T(8,128)(2,1)} %bitcast.9, bf16[128,512]{1,0:T(8,128)(2,1)} %kn_hbm.1, bf16[64,128]{1,0:T(8,128)(2,1)} %bitcast.11, ...), custom_call_target="tpu_custom_call" | custom-call | tf_op jit(solution)/shard_map/pallas_call | solution.py:267
  31.6 0.0 copy-start
  31.6 0.0 copy-start.1
  31.7 0.0 copy-start.2
  31.7 3.1 %copy.14 = bf16[128,16,512]{2,1,0:T(8,128)(2,1)} copy(bf16[128,16,512]{2,1,0:T(8,128)(2,1)} %bitcast.8) | data formatting | bytes 4194304
  34.8 0.0 copy-done
  34.8 0.7 %copy.15 = bf16[128,16,64]{0,2,1:T(8,128)(2,1)} copy(bf16[128,16,64]{0,2,1:T(8,128)(2,1)S(1)} %bitcast.10) | data formatting | bytes 524288
  35.5 0.0 copy-done.1
  35.5 0.7 %copy.16 = f32[64,512]{1,0:T(8,128)} copy(f32[64,512]{1,0:T(8,128)S(1)} %copy-done.1) | data formatting | bytes 262144
  36.2 0.0 copy-done.2
  36.2 0.6 %copy.17 = f32[64,64]{1,0:T(8,128)} copy(f32[64,64]{1,0:T(8,128)S(1)} %copy-done.2) | data formatting | bytes 32768
Async XLA Ops:
  31.6 3.2 %copy-start = (bf16[16,64,128]{2,1,0:T(8,128)(2,1)S(1)}, bf16[16,64,128]{2,1,0:T(8,128)(2,1)}, u32[]{:S(2)}) copy-start(bf16[16,64,128]{2,1,0:T(8,128)(2,1)} %get-tuple-element.9) | copy-start | bytes 786436
  31.6 3.9 %copy-start.1 = (f32[64,512]{1,0:T(8,128)S(1)}, f32[64,512]{1,0:T(8,128)}, u32[]{:S(2)}) copy-start(f32[64,512]{1,0:T(8,128)} %get-tuple-element.18) | copy-start | bytes 393220
  31.7 4.5 %copy-start.2 = (f32[64,64]{1,0:T(8,128)S(1)}, f32[64,64]{1,0:T(8,128)}, u32[]{:S(2)}) copy-start(f32[64,64]{1,0:T(8,128)} %get-tuple-element.19) | copy-start | bytes 49156

commit v3 on v2

--- a/solution.py
+++ b/solution.py
@@ -10,6 +10,7 @@
 
 WINDOW = 4
 PAIRS = WINDOW // 2
+ORDER = (0, 2, 1, 3)
 SCORE_SCALE = 192.0 ** (-0.5)
 LOG2E = math.log2(math.e)
 LANES = 128
@@ -57,12 +58,15 @@
     ds_ref,
     bias_ref,
     acc_ref,
+    comb_out,
+    comb_in,
     dk_out,
     dk_in,
     load_sem,
     store_sem,
     k_send,
     k_recv,
+    c_sem,
     d_send,
     d_recv,
 ):
@@ -90,16 +94,22 @@
     load_kn.start()
     load_kr.start()
 
+    core = lax.rem(c, 2)
+    sibling = c + 1 - 2 * core
+    ahead = lax.rem(c + 2, n_ctx)
+    behind = lax.rem(c + n_ctx - 2, n_ctx)
+    far = lax.rem(c + n_ctx - 3 + 6 * core, n_ctx)
+
     barrier = pltpu.get_barrier_semaphore()
     greeted = 0
-    for d in range(1 - WINDOW, WINDOW):
+    for where in (c, sibling, ahead, behind, far):
         for k in range(n_hg):
-            if d == 0 and k == 0:
+            if where is c and k == 0:
                 continue
             pl.semaphore_signal(
                 barrier,
                 inc=1,
-                device_id=(lax.rem(c + d + n_ctx, n_ctx), lax.rem(h + k, n_hg)),
+                device_id=(where, lax.rem(h + k, n_hg)),
                 device_id_type=MESH,
             )
             greeted += 1
@@ -111,31 +121,38 @@
     load_kr.wait()
     pl.semaphore_wait(barrier, greeted)
 
-    sends = []
-    for d in range(1, WINDOW):
-        both = []
-        for part, buffer in enumerate((kn_all, krt_all)):
-            copy = pltpu.make_async_remote_copy(
-                src_ref=buffer.at[0],
-                dst_ref=buffer.at[d],
-                send_sem=k_send.at[d, part],
-                recv_sem=k_recv.at[d, part],
-                device_id=(lax.rem(c + d, n_ctx), h),
+    def latent_copy(source, place, target, kind):
+        return [
+            pltpu.make_async_remote_copy(
+                src_ref=buffer.at[source],
+                dst_ref=buffer.at[place],
+                send_sem=k_send.at[kind, part],
+                recv_sem=k_recv.at[place, part],
+                device_id=(target, h),
                 device_id_type=MESH,
             )
-            copy.start()
-            both.append(copy)
-        sends.append(both)
+            for part, buffer in enumerate((kn_all, krt_all))
+        ]
+
+    to_ahead = latent_copy(0, 1, ahead, 0)
+    to_other = latent_copy(0, 2 + core, lax.rem(c + 1 + 2 * core, n_ctx), 1)
+    handed_on = latent_copy(1, 3 - core, sibling, 2)
+    for copy in to_ahead + to_other:
+        copy.start()
+
+    def wait_latents(place):
+        for copy in latent_copy(0, place, sibling, 0):
+            copy.wait_recv()
 
     key_block = lax.broadcasted_iota(jnp.int32, (1, WINDOW * keys), 1) // (keys // blocks)
     for rb in range(blocks):
         bias = jnp.zeros((1, WINDOW * keys), jnp.float32)
-        for d in range(WINDOW):
+        for place, d in enumerate(ORDER):
             source = lax.rem(c - d + n_ctx, n_ctx)
             for kb in range(blocks):
                 bit = mask_ref[c * blocks + rb, source * blocks + kb]
                 value = jnp.where(bit == 1, 0.0, -jnp.inf).astype(jnp.float32)
-                bias = jnp.where(key_block == d * blocks + kb, value, bias)
+                bias = jnp.where(key_block == place * blocks + kb, value, bias)
         bias_ref[rb : rb + 1, :] = bias
 
     acc_ref[...] = jnp.zeros_like(acc_ref)
@@ -148,10 +165,13 @@
     load_g.wait()
 
     for p in range(PAIRS):
-        for d in (2 * p, 2 * p + 1):
-            if d > 0:
-                for copy in sends[d - 1]:
-                    copy.wait_recv()
+        if p == 0:
+            wait_latents(1)
+            for copy in handed_on:
+                copy.start()
+        else:
+            wait_latents(2)
+            wait_latents(3)
         cols = slice(p * pair, (p + 1) * pair)
 
         def score_tile(i, _, p=p, cols=cols):
@@ -171,26 +191,29 @@
         acc_ref[p, :, :latent] += dot_tn(ds, q) + dot_tn(prob, g_ref[r, :])
         acc_ref[p, :, latent : latent + rope] += dot_tn(ds, qr_ref[r, :])
 
-    def send_key_grads(p):
+    def send_pieces(kind, target):
         out = []
-        for d in (2 * p + 1, 2 * p):
-            block = acc_ref[p, (d - 2 * p) * keys : (d - 2 * p + 1) * keys, :]
-            dk_out[d] = block.reshape(n_hg, piece, block.shape[1]).astype(dk_out.dtype)
-            for k in reversed(range(n_hg)):
-                if d == 0 and k == 0:
-                    continue
-                peer = lax.rem(h + k, n_hg)
-                copy = pltpu.make_async_remote_copy(
-                    src_ref=dk_out.at[d, peer],
-                    dst_ref=dk_in.at[d, k],
-                    send_sem=d_send.at[d, k],
-                    recv_sem=d_recv.at[d, k],
-                    device_id=(lax.rem(c - d + n_ctx, n_ctx), peer),
-                    device_id_type=MESH,
-                )
-                copy.start()
-                out.append((d, k, copy))
+        for k in reversed(range(n_hg)):
+            if kind == 0 and k == 0:
+                continue
+            peer = lax.rem(h + k, n_hg)
+            copy = pltpu.make_async_remote_copy(
+                src_ref=dk_out.at[kind, peer],
+                dst_ref=dk_in.at[kind, k],
+                send_sem=d_send.at[kind, k],
+                recv_sem=d_recv.at[kind, k],
+                device_id=(target, peer),
+                device_id_type=MESH,
+            )
+            copy.start()
+            out.append((kind, k, copy))
         return out
+
+    def split(block):
+        return block.reshape(n_hg, piece, block.shape[1]).astype(dk_out.dtype)
+
+    def half_of_last(which):
+        return acc_ref[last, pl.ds(pl.multiple_of(which * keys, keys), keys), :]
 
     last = PAIRS - 1
 
@@ -207,7 +230,18 @@
         r = slice(start, start + soft_rows)
         cols = slice(last * pair, (last + 1) * pair)
         add_key_grads(last, r, ds_ref[r, cols], prob_ref[r, cols])
-    moving = send_key_grads(last)
+    comb_out[...] = half_of_last(core).astype(comb_out.dtype)
+    combine = pltpu.make_async_remote_copy(
+        src_ref=comb_out,
+        dst_ref=comb_in,
+        send_sem=c_sem.at[0],
+        recv_sem=c_sem.at[1],
+        device_id=(sibling, h),
+        device_id_type=MESH,
+    )
+    combine.start()
+    dk_out[2] = split(half_of_last(1 - core))
+    moving = send_pieces(2, lax.rem(c + n_ctx - 3 + 2 * core, n_ctx))
 
     for p in reversed(range(last)):
         cols = slice(p * pair, (p + 1) * pair)
@@ -218,7 +252,12 @@
             return 0
 
         lax.fori_loop(0, tiles, grad_tile, 0)
-        moving += send_key_grads(p)
+
+    combine.wait_recv()
+    dk_out[1] = split(acc_ref[0, keys:, :] + comb_in[...].astype(jnp.float32))
+    moving += send_pieces(1, behind)
+    dk_out[0] = split(acc_ref[0, :keys, :])
+    moving += send_pieces(0, c)
 
     stores = []
     for i in range(tiles):
@@ -239,19 +278,37 @@
     stores.append(copy)
 
     total = acc_ref[0, pl.ds(pl.multiple_of(h * piece, piece), piece), :]
-    for d, k, copy in sorted(moving, key=lambda m: (-m[0], m[1])):
+    for kind, k, copy in sorted(moving, key=lambda m: (-m[0], m[1])):
         copy.wait_recv()
-        total = total + dk_in[d, k].astype(jnp.float32)
+        total = total + dk_in[kind, k].astype(jnp.float32)
     dkn_ref[...] = total[:, :latent]
     dkr_ref[...] = total[:, latent : latent + rope]
 
-    for both in sends:
-        for copy in both:
-            copy.wait_send()
+    for copy in to_ahead + to_other + handed_on + [combine]:
+        copy.wait_send()
     for copy in stores:
         copy.wait()
     for _, _, copy in moving:
         copy.wait_send()
+
+
+def hand_over(dq_in, dqr_in, dkn_in, dkr_in, dq_ref, dqr_ref, dkn_ref, dkr_ref, dq, dqr, dkn, dkr, load_sem, store_sem):
+    parts = []
+    rows = dq.shape[0]
+    step = rows // 4
+    for at in range(0, rows, step):
+        r = pl.ds(at, step)
+        parts.append((dq_in.at[r, :], dq.at[r, :], dq_ref.at[r, :]))
+    parts += [(dqr_in, dqr, dqr_ref), (dkn_in, dkn, dkn_ref), (dkr_in, dkr, dkr_ref)]
+    loads = [pltpu.make_async_copy(a, b, load_sem.at[i]) for i, (a, b, _) in enumerate(parts)]
+    stores = [pltpu.make_async_copy(b, o, store_sem.at[i]) for i, (_, b, o) in enumerate(parts)]
+    for load in loads:
+        load.start()
+    for load, store in zip(loads, stores):
+        load.wait()
+        store.start()
+    for store in stores:
+        store.wait()
 
 
 def on_device(n_ctx, n_hg, q, qr, kn, kr, g, block_mask):
@@ -291,19 +348,32 @@
             pltpu.VMEM((rows, WINDOW * tokens), bf16),
             pltpu.VMEM((blocks, WINDOW * tokens), f32),
             pltpu.VMEM((PAIRS, 2 * tokens, width), f32),
-            pltpu.VMEM((WINDOW, n_hg, piece, width), bf16),
-            pltpu.VMEM((WINDOW, n_hg, piece, width), bf16),
+            pltpu.VMEM((tokens, width), bf16),
+            pltpu.VMEM((tokens, width), bf16),
+            pltpu.VMEM((3, n_hg, piece, width), bf16),
+            pltpu.VMEM((3, n_hg, piece, width), bf16),
             pltpu.SemaphoreType.DMA((5,)),
             pltpu.SemaphoreType.DMA((rows // 512 + 1,)),
             pltpu.SemaphoreType.DMA((WINDOW, 2)),
             pltpu.SemaphoreType.DMA((WINDOW, 2)),
-            pltpu.SemaphoreType.DMA((WINDOW, n_hg)),
-            pltpu.SemaphoreType.DMA((WINDOW, n_hg)),
+            pltpu.SemaphoreType.DMA((2,)),
+            pltpu.SemaphoreType.DMA((3, n_hg)),
+            pltpu.SemaphoreType.DMA((3, n_hg)),
         ],
         compiler_params=pltpu.CompilerParams(
             collective_id=0, has_side_effects=True, vmem_limit_bytes=60 * 1024 * 1024
         ),
     )(block_mask, q.reshape(rows, latent), qr.transpose(1, 2, 0), kn, kr.T, g.reshape(rows, latent))
+    made = (dq, dqr, dkn, dkr)
+    dq, dqr, dkn, dkr = pl.pallas_call(
+        hand_over,
+        out_shape=tuple(jax.ShapeDtypeStruct(a.shape, a.dtype) for a in made),
+        in_specs=[hbm] * 4,
+        out_specs=[hbm] * 4,
+        scratch_shapes=[pltpu.VMEM(a.shape, a.dtype) for a in made]
+        + [pltpu.SemaphoreType.DMA((7,)), pltpu.SemaphoreType.DMA((7,))],
+        compiler_params=pltpu.CompilerParams(vmem_limit_bytes=60 * 1024 * 1024),
+    )(*made)
     return dq.reshape(tokens, heads, latent), dqr.transpose(2, 0, 1), dkn, dkr
 
 

time: 37 us -> 31.6 us (0.85)
  the two profiles are of different devices: /device:TPU:1 before, /device:TPU:0 now
where the time goes in v3:
time: 31.6 us; the launch traced here: 31.4 us
  Pallas kernels  30.7 us (97%)
  between operations  0.64 us (2%)
    pallas_call x1, Pallas kernels, on_device(): pl.pallas_call(functools.partial(kernel, n_ctx, n_hg), out_shape=(jax.Sha...  28.1 us
    pallas_call x1, Pallas kernels, on_device(): pl.pallas_call(hand_over, out_shape=tuple((jax.ShapeDtypeStruct(a.shape,...  2.6 us

profile of v3, /device:TPU:0, one launch (start us, length us, event | category | flops | bytes accessed | tf_op | source)
XLA Modules:
  0.0 31.4 jit_solution(5335854818387279666)
XLA Ops:
  0.6 28.1 %shard_map.93 = (bf16[2048,512]{1,0:T(8,128)(2,1)}, bf16[16,64,128]{2,1,0:T(8,128)(2,1)}, f32[64,512]{1,0:T(8,128)}, f32[64,64]{1,0:T(8,128)}) custom-call(s32[32,32]{1,0:T(8,128)} %mask_ref.1, bf16[2048,512]{1,0:T(8,128)(2,1)} %bitcast.6, bf16[16,64,128]{2,1,0:T(8,128)(2,1)} %bitcast.8, bf16[128,512]{1,0:T(8,128)(2,1)} %kn_hbm.1, bf16[64,128]{1,0:T(8,128)(2,1)} %bitcast.9, ...), custom_call_target="tpu_custom_call" | custom-call | tf_op jit(solution)/shard_map/pallas_call | solution.py:324
  28.8 2.6 %shard_map.94 = (bf16[2048,512]{1,0:T(8,128)(2,1)}, bf16[16,64,128]{2,1,0:T(8,128)(2,1)}, f32[64,512]{1,0:T(8,128)}, f32[64,64]{1,0:T(8,128)}) custom-call(bf16[2048,512]{1,0:T(8,128)(2,1)} %get-tuple-element.12.dq_in, bf16[16,64,128]{2,1,0:T(8,128)(2,1)} %get-tuple-element.13.dqr_in, f32[64,512]{1,0:T(8,128)} %get-tuple-element.14.dkn_in, ...), custom_call_target="tpu_custom_call" | custom-call | tf_op jit(solution)/shard_map/pallas_call | solution.py:368

commit v4 on v3

--- a/solution.py
+++ b/solution.py
@@ -49,6 +49,7 @@
     g_ref,
     kn_all,
     krt_all,
+    kr_all,
     dq_tile,
     dqr_wide,
     dqrt_ref,
@@ -56,7 +57,7 @@
     dp_ref,
     prob_ref,
     ds_ref,
-    bias_ref,
+    top_ref,
     acc_ref,
     comb_out,
     comb_in,
@@ -81,8 +82,8 @@
     block_rows = rows // blocks
     tile = 512
     tiles = rows // tile
-    soft_rows = 256
-    sub_rows = 32
+    group = 256
+    chunk = keys // blocks
     c = lax.axis_index("ctx")
     h = lax.axis_index("hg")
 
@@ -144,16 +145,13 @@
         for copy in latent_copy(0, place, sibling, 0):
             copy.wait_recv()
 
-    key_block = lax.broadcasted_iota(jnp.int32, (1, WINDOW * keys), 1) // (keys // blocks)
+    bias = []
     for rb in range(blocks):
-        bias = jnp.zeros((1, WINDOW * keys), jnp.float32)
         for place, d in enumerate(ORDER):
             source = lax.rem(c - d + n_ctx, n_ctx)
             for kb in range(blocks):
                 bit = mask_ref[c * blocks + rb, source * blocks + kb]
-                value = jnp.where(bit == 1, 0.0, -jnp.inf).astype(jnp.float32)
-                bias = jnp.where(key_block == place * blocks + kb, value, bias)
-        bias_ref[rb : rb + 1, :] = bias
+                bias.append(jnp.where(bit == 1, 0.0, -jnp.inf).astype(jnp.float32))
 
     acc_ref[...] = jnp.zeros_like(acc_ref)
     load_qr.wait()
@@ -164,32 +162,41 @@
     load_q.wait()
     load_g.wait()
 
+    def turn_rope(place):
+        kr_all[place] = krt_all[place].astype(jnp.float32).T.astype(kr_all.dtype)
+
+    turn_rope(0)
     for p in range(PAIRS):
         if p == 0:
             wait_latents(1)
             for copy in handed_on:
                 copy.start()
+            turn_rope(1)
         else:
-            wait_latents(2)
-            wait_latents(3)
-        cols = slice(p * pair, (p + 1) * pair)
-
-        def score_tile(i, _, p=p, cols=cols):
-            r = pl.ds(pl.multiple_of(i * tile, tile), tile)
-            kn = kn_all[2 * p : 2 * p + 2].reshape(pair, latent)
-            krt = jnp.concatenate([krt_all[2 * p], krt_all[2 * p + 1]], axis=1)
-            bias = bias_ref[pl.ds(i * tile // block_rows, 1), cols]
-            s = dot_nt(q_ref[r, :], kn) + dot_nn(qr_ref[r, :], krt)
-            x_ref[r, cols] = s * (SCORE_SCALE * LOG2E) + bias
-            dp_ref[r, cols] = dot_nt(g_ref[r, :], kn)
-            return 0
-
-        lax.fori_loop(0, tiles, score_tile, 0)
-
-    def add_key_grads(p, r, ds, prob):
-        q = q_ref[r, :]
-        acc_ref[p, :, :latent] += dot_tn(ds, q) + dot_tn(prob, g_ref[r, :])
-        acc_ref[p, :, latent : latent + rope] += dot_tn(ds, qr_ref[r, :])
+            for place in (2, 3):
+                wait_latents(place)
+                turn_rope(place)
+        kn = kn_all[2 * p : 2 * p + 2].reshape(pair, latent)
+        kr = kr_all[2 * p : 2 * p + 2].reshape(pair, rope)
+        for i in range(tiles):
+            r = slice(i * tile, (i + 1) * tile)
+            rb = i * tile // block_rows
+            s = dot_nt(kn, q_ref[r, :]) + dot_nt(kr, qr_ref[r, :])
+            top = None
+            for j in range(pair // chunk):
+                number = (rb * WINDOW + 2 * p) * blocks + j
+                x = s[j * chunk : (j + 1) * chunk, :] * (SCORE_SCALE * LOG2E) + bias[number]
+                x_ref[p * pair + j * chunk : p * pair + (j + 1) * chunk, r] = x
+                part = jnp.max(x.reshape(chunk // 8, 8, tile), axis=0)
+                top = part if top is None else jnp.maximum(top, part)
+            top_ref[8 * p : 8 * p + 8, r] = top
+            dp_ref[p * pair : (p + 1) * pair, r] = dot_nt(kn, g_ref[r, :])
+
+    def add_key_grads(p, r):
+        ds = ds_ref[p * pair : (p + 1) * pair, r]
+        prob = prob_ref[p * pair : (p + 1) * pair, r]
+        acc_ref[p, :, :latent] += dot_nn(ds, q_ref[r, :]) + dot_nn(prob, g_ref[r, :])
+        acc_ref[p, :, latent : latent + rope] += dot_nn(ds, qr_ref[r, :])
 
     def send_pieces(kind, target):
         out = []
@@ -217,19 +224,29 @@
 
     last = PAIRS - 1
 
-    for start in range(0, rows, soft_rows):
-        for at in range(start, start + soft_rows, sub_rows):
-            r = slice(at, at + sub_rows)
-            x = x_ref[r, :]
-            dp = dp_ref[r, :]
-            e = jnp.exp2(x - jnp.max(x, axis=1, keepdims=True))
-            inv = 1.0 / jnp.sum(e, axis=1, keepdims=True)
-            delta = jnp.sum(e * dp, axis=1, keepdims=True) * inv
-            prob_ref[r, :] = (e * inv).astype(jnp.bfloat16)
-            ds_ref[r, :] = (e * (inv * SCORE_SCALE) * (dp - delta)).astype(jnp.bfloat16)
-        r = slice(start, start + soft_rows)
-        cols = slice(last * pair, (last + 1) * pair)
-        add_key_grads(last, r, ds_ref[r, cols], prob_ref[r, cols])
+    def folded(a):
+        return jnp.sum(a.reshape(a.shape[0] // 8, 8, a.shape[1]), axis=0)
+
+    for start in range(0, rows, tile):
+        for at in range(start, start + tile, group):
+            r = slice(at, at + group)
+            top = jnp.max(top_ref[:, r], axis=0, keepdims=True)
+            total = jnp.zeros((8, group), jnp.float32)
+            mixed = jnp.zeros((8, group), jnp.float32)
+            for k in range(0, WINDOW * keys, chunk):
+                e = jnp.exp2(x_ref[k : k + chunk, r] - top)
+                x_ref[k : k + chunk, r] = e
+                total += folded(e)
+                mixed += folded(e * dp_ref[k : k + chunk, r])
+            inv = 1.0 / jnp.sum(total, axis=0, keepdims=True)
+            delta = jnp.sum(mixed, axis=0, keepdims=True) * inv
+            scaled = inv * SCORE_SCALE
+            for k in range(0, WINDOW * keys, chunk):
+                e = x_ref[k : k + chunk, r]
+                prob_ref[k : k + chunk, r] = (e * inv).astype(jnp.bfloat16)
+                ds = (e * scaled) * (dp_ref[k : k + chunk, r] - delta)
+                ds_ref[k : k + chunk, r] = ds.astype(jnp.bfloat16)
+        add_key_grads(last, slice(start, start + tile))
     comb_out[...] = half_of_last(core).astype(comb_out.dtype)
     combine = pltpu.make_async_remote_copy(
         src_ref=comb_out,
@@ -244,14 +261,8 @@
     moving = send_pieces(2, lax.rem(c + n_ctx - 3 + 2 * core, n_ctx))
 
     for p in reversed(range(last)):
-        cols = slice(p * pair, (p + 1) * pair)
-
-        def grad_tile(i, _, p=p, cols=cols):
-            r = pl.ds(pl.multiple_of(i * tile, tile), tile)
-            add_key_grads(p, r, ds_ref[r, cols], prob_ref[r, cols])
-            return 0
-
-        lax.fori_loop(0, tiles, grad_tile, 0)
+        for start in range(0, rows, 2 * tile):
+            add_key_grads(p, slice(start, start + 2 * tile))
 
     combine.wait_recv()
     dk_out[1] = split(acc_ref[0, keys:, :] + comb_in[...].astype(jnp.float32))
@@ -262,11 +273,9 @@
     stores = []
     for i in range(tiles):
         r = slice(i * tile, (i + 1) * tile)
-        ds = ds_ref[r, :]
-        kn = kn_all[...].reshape(WINDOW * keys, latent)
-        krt = jnp.concatenate([krt_all[d] for d in range(WINDOW)], axis=1)
-        dq_tile[r, :] = dot_nn(ds, kn).astype(dq_tile.dtype)
-        dqr_wide[r, :] = dot_nt(ds, krt)
+        ds = ds_ref[:, r]
+        dq_tile[r, :] = dot_tn(ds, kn_all[...].reshape(WINDOW * keys, latent)).astype(dq_tile.dtype)
+        dqr_wide[r, :] = dot_tn(ds, kr_all[...].reshape(WINDOW * keys, rope))
         copy = pltpu.make_async_copy(dq_tile.at[r, :], dq_ref.at[r, :], store_sem.at[i])
         copy.start()
         stores.append(copy)
@@ -339,14 +348,15 @@
             pltpu.VMEM((rows, latent), bf16),
             pltpu.VMEM((WINDOW, tokens, latent), bf16),
             pltpu.VMEM((WINDOW, rope, tokens), bf16),
+            pltpu.VMEM((WINDOW, tokens, rope), bf16),
             pltpu.VMEM((rows, latent), bf16),
             pltpu.VMEM((rows, rope), f32),
             pltpu.VMEM((heads, rope, tokens), bf16),
-            pltpu.VMEM((rows, WINDOW * tokens), f32),
-            pltpu.VMEM((rows, WINDOW * tokens), f32),
-            pltpu.VMEM((rows, WINDOW * tokens), bf16),
-            pltpu.VMEM((rows, WINDOW * tokens), bf16),
-            pltpu.VMEM((blocks, WINDOW * tokens), f32),
+            pltpu.VMEM((WINDOW * tokens, rows), f32),
+            pltpu.VMEM((WINDOW * tokens, rows), f32),
+            pltpu.VMEM((WINDOW * tokens, rows), bf16),
+            pltpu.VMEM((WINDOW * tokens, rows), bf16),
+            pltpu.VMEM((8 * PAIRS, rows), f32),
             pltpu.VMEM((PAIRS, 2 * tokens, width), f32),
             pltpu.VMEM((tokens, width), bf16),
             pltpu.VMEM((tokens, width), bf16),

time: 31.6 us -> 29.7 us (0.940)
  Pallas kernels: 30.7 us -> 28.8 us
    pallas_call x1, Pallas kernels: 28.1 us -> 26.2 us  [on_device(): pl.pallas_call(functools.partial(kernel, n_ctx, n_hg), out_shape=(jax.Sha...]
where the time goes in v4:
time: 29.7 us; the launch traced here: 29.5 us
  Pallas kernels  28.8 us (97%)
  between operations  0.64 us (2%)
    pallas_call x1, Pallas kernels, on_device(): pl.pallas_call(functools.partial(kernel, n_ctx, n_hg), out_shape=(jax.Sha...  26.2 us
    pallas_call x1, Pallas kernels, on_device(): pl.pallas_call(hand_over, out_shape=tuple((jax.ShapeDtypeStruct(a.shape,...  2.6 us

profile of v4, /device:TPU:0, one launch (start us, length us, event | category | flops | bytes accessed | tf_op | source)
XLA Modules:
  0.0 29.5 jit_solution(9660544591830708859)
XLA Ops:
  0.6 26.2 %shard_map.93 = (bf16[2048,512]{1,0:T(8,128)(2,1)}, bf16[16,64,128]{2,1,0:T(8,128)(2,1)}, f32[64,512]{1,0:T(8,128)}, f32[64,64]{1,0:T(8,128)}) custom-call(s32[32,32]{1,0:T(8,128)} %mask_ref.1, bf16[2048,512]{1,0:T(8,128)(2,1)} %bitcast.6, bf16[16,64,128]{2,1,0:T(8,128)(2,1)} %bitcast.8, bf16[128,512]{1,0:T(8,128)(2,1)} %kn_hbm.1, bf16[64,128]{1,0:T(8,128)(2,1)} %bitcast.9, ...), custom_call_target="tpu_custom_call" | custom-call | tf_op jit(solution)/shard_map/pallas_call | solution.py:333
  26.9 2.6 %shard_map.94 = (bf16[2048,512]{1,0:T(8,128)(2,1)}, bf16[16,64,128]{2,1,0:T(8,128)(2,1)}, f32[64,512]{1,0:T(8,128)}, f32[64,64]{1,0:T(8,128)}) custom-call(bf16[2048,512]{1,0:T(8,128)(2,1)} %get-tuple-element.12.dq_in, bf16[16,64,128]{2,1,0:T(8,128)(2,1)} %get-tuple-element.13.dqr_in, f32[64,512]{1,0:T(8,128)} %get-tuple-element.14.dkn_in, ...), custom_call_target="tpu_custom_call" | custom-call | tf_op jit(solution)/shard_map/pallas_call | solution.py:378

commit v5 on v4

--- a/solution.py
+++ b/solution.py
@@ -192,11 +192,10 @@
             top_ref[8 * p : 8 * p + 8, r] = top
             dp_ref[p * pair : (p + 1) * pair, r] = dot_nt(kn, g_ref[r, :])
 
-    def add_key_grads(p, r):
-        ds = ds_ref[p * pair : (p + 1) * pair, r]
-        prob = prob_ref[p * pair : (p + 1) * pair, r]
-        acc_ref[p, :, :latent] += dot_nn(ds, q_ref[r, :]) + dot_nn(prob, g_ref[r, :])
-        acc_ref[p, :, latent : latent + rope] += dot_nn(ds, qr_ref[r, :])
+    def add_key_grads(r):
+        ds = ds_ref[:, r]
+        acc_ref[:, :latent] += dot_nn(ds, q_ref[r, :]) + dot_nn(prob_ref[:, r], g_ref[r, :])
+        acc_ref[:, latent : latent + rope] += dot_nn(ds, qr_ref[r, :])
 
     def send_pieces(kind, target):
         out = []
@@ -219,10 +218,8 @@
     def split(block):
         return block.reshape(n_hg, piece, block.shape[1]).astype(dk_out.dtype)
 
-    def half_of_last(which):
-        return acc_ref[last, pl.ds(pl.multiple_of(which * keys, keys), keys), :]
-
-    last = PAIRS - 1
+    def one_of_last(which):
+        return acc_ref[pl.ds(pl.multiple_of(pair + which * keys, keys), keys), :]
 
     def folded(a):
         return jnp.sum(a.reshape(a.shape[0] // 8, 8, a.shape[1]), axis=0)
@@ -246,8 +243,10 @@
                 prob_ref[k : k + chunk, r] = (e * inv).astype(jnp.bfloat16)
                 ds = (e * scaled) * (dp_ref[k : k + chunk, r] - delta)
                 ds_ref[k : k + chunk, r] = ds.astype(jnp.bfloat16)
-        add_key_grads(last, slice(start, start + tile))
-    comb_out[...] = half_of_last(core).astype(comb_out.dtype)
+        if start > 0:
+            add_key_grads(slice(start - tile, start))
+    add_key_grads(slice(rows - tile, rows))
+    comb_out[...] = one_of_last(core).astype(comb_out.dtype)
     combine = pltpu.make_async_remote_copy(
         src_ref=comb_out,
         dst_ref=comb_in,
@@ -257,18 +256,14 @@
         device_id_type=MESH,
     )
     combine.start()
-    dk_out[2] = split(half_of_last(1 - core))
+    dk_out[2] = split(one_of_last(1 - core))
     moving = send_pieces(2, lax.rem(c + n_ctx - 3 + 2 * core, n_ctx))
 
-    for p in reversed(range(last)):
-        for start in range(0, rows, 2 * tile):
-            add_key_grads(p, slice(start, start + 2 * tile))
-
+    dk_out[0] = split(acc_ref[:keys, :])
+    moving += send_pieces(0, c)
     combine.wait_recv()
-    dk_out[1] = split(acc_ref[0, keys:, :] + comb_in[...].astype(jnp.float32))
+    dk_out[1] = split(acc_ref[keys:pair, :] + comb_in[...].astype(jnp.float32))
     moving += send_pieces(1, behind)
-    dk_out[0] = split(acc_ref[0, :keys, :])
-    moving += send_pieces(0, c)
 
     stores = []
     for i in range(tiles):
@@ -286,7 +281,7 @@
     copy.start()
     stores.append(copy)
 
-    total = acc_ref[0, pl.ds(pl.multiple_of(h * piece, piece), piece), :]
+    total = acc_ref[pl.ds(pl.multiple_of(h * piece, piece), piece), :]
     for kind, k, copy in sorted(moving, key=lambda m: (-m[0], m[1])):
         copy.wait_recv()
         total = total + dk_in[kind, k].astype(jnp.float32)
@@ -357,7 +352,7 @@
             pltpu.VMEM((WINDOW * tokens, rows), bf16),
             pltpu.VMEM((WINDOW * tokens, rows), bf16),
             pltpu.VMEM((8 * PAIRS, rows), f32),
-            pltpu.VMEM((PAIRS, 2 * tokens, width), f32),
+            pltpu.VMEM((WINDOW * tokens, width), f32),
             pltpu.VMEM((tokens, width), bf16),
             pltpu.VMEM((tokens, width), bf16),
             pltpu.VMEM((3, n_hg, piece, width), bf16),

time: 29.7 us -> 30.8 us (1.037)
  Pallas kernels: 28.8 us -> 29.9 us
    pallas_call x1, Pallas kernels: 26.2 us -> 27.3 us  [on_device(): pl.pallas_call(functools.partial(kernel, n_ctx, n_hg), out_shape=(jax.Sha...]
where the time goes in v5:
time: 30.8 us; the launch traced here: 30.6 us
  Pallas kernels  29.9 us (97%)
  between operations  0.64 us (2%)
    pallas_call x1, Pallas kernels, on_device(): pl.pallas_call(functools.partial(kernel, n_ctx, n_hg), out_shape=(jax.Sha...  27.3 us
    pallas_call x1, Pallas kernels, on_device(): pl.pallas_call(hand_over, out_shape=tuple((jax.ShapeDtypeStruct(a.shape,...  2.6 us

profile of v5, /device:TPU:0, one launch (start us, length us, event | category | flops | bytes accessed | tf_op | source)
XLA Modules:
  0.0 30.6 jit_solution(13377400151790291198)
XLA Ops:
  0.6 27.3 %shard_map.93 = (bf16[2048,512]{1,0:T(8,128)(2,1)}, bf16[16,64,128]{2,1,0:T(8,128)(2,1)}, f32[64,512]{1,0:T(8,128)}, f32[64,64]{1,0:T(8,128)}) custom-call(s32[32,32]{1,0:T(8,128)} %mask_ref.1, bf16[2048,512]{1,0:T(8,128)(2,1)} %bitcast.6, bf16[16,64,128]{2,1,0:T(8,128)(2,1)} %bitcast.8, bf16[128,512]{1,0:T(8,128)(2,1)} %kn_hbm.1, bf16[64,128]{1,0:T(8,128)(2,1)} %bitcast.9, ...), custom_call_target="tpu_custom_call" | custom-call | tf_op jit(solution)/shard_map/pallas_call | solution.py:328
  28.0 2.6 %shard_map.94 = (bf16[2048,512]{1,0:T(8,128)(2,1)}, bf16[16,64,128]{2,1,0:T(8,128)(2,1)}, f32[64,512]{1,0:T(8,128)}, f32[64,64]{1,0:T(8,128)}) custom-call(bf16[2048,512]{1,0:T(8,128)(2,1)} %get-tuple-element.12.dq_in, bf16[16,64,128]{2,1,0:T(8,128)(2,1)} %get-tuple-element.13.dqr_in, f32[64,512]{1,0:T(8,128)} %get-tuple-element.14.dkn_in, ...), custom_call_target="tpu_custom_call" | custom-call | tf_op jit(solution)/shard_map/pallas_call | solution.py:373

commit v6 on v5

--- a/solution.py
+++ b/solution.py
@@ -9,7 +9,7 @@
 from jax.sharding import PartitionSpec as P
 
 WINDOW = 4
-PAIRS = WINDOW // 2
+PHASES = ((0, 1), (1, 1), (2, 2))
 ORDER = (0, 2, 1, 3)
 SCORE_SCALE = 192.0 ** (-0.5)
 LOG2E = math.log2(math.e)
@@ -77,7 +77,6 @@
     tokens = qrt_ref.shape[2]
     keys = kn_all.shape[1]
     piece = keys // n_hg
-    pair = 2 * keys
     blocks = mask_ref.shape[0] // n_ctx
     block_rows = rows // blocks
     tile = 512
@@ -166,36 +165,37 @@
         kr_all[place] = krt_all[place].astype(jnp.float32).T.astype(kr_all.dtype)
 
     turn_rope(0)
-    for p in range(PAIRS):
-        if p == 0:
-            wait_latents(1)
-            for copy in handed_on:
-                copy.start()
-            turn_rope(1)
-        else:
-            for place in (2, 3):
-                wait_latents(place)
-                turn_rope(place)
-        kn = kn_all[2 * p : 2 * p + 2].reshape(pair, latent)
-        kr = kr_all[2 * p : 2 * p + 2].reshape(pair, rope)
+    for phase, (first, count) in enumerate(PHASES):
+        for place in range(first, first + count):
+            if place == 0:
+                continue
+            wait_latents(place)
+            if place == 1:
+                for copy in handed_on:
+                    copy.start()
+            turn_rope(place)
+        here = count * keys
+        kn = kn_all[first : first + count].reshape(here, latent)
+        kr = kr_all[first : first + count].reshape(here, rope)
         for i in range(tiles):
             r = slice(i * tile, (i + 1) * tile)
             rb = i * tile // block_rows
             s = dot_nt(kn, q_ref[r, :]) + dot_nt(kr, qr_ref[r, :])
             top = None
-            for j in range(pair // chunk):
-                number = (rb * WINDOW + 2 * p) * blocks + j
+            for j in range(here // chunk):
+                number = (rb * WINDOW + first) * blocks + j
                 x = s[j * chunk : (j + 1) * chunk, :] * (SCORE_SCALE * LOG2E) + bias[number]
-                x_ref[p * pair + j * chunk : p * pair + (j + 1) * chunk, r] = x
+                x_ref[first * keys + j * chunk : first * keys + (j + 1) * chunk, r] = x
                 part = jnp.max(x.reshape(chunk // 8, 8, tile), axis=0)
                 top = part if top is None else jnp.maximum(top, part)
-            top_ref[8 * p : 8 * p + 8, r] = top
-            dp_ref[p * pair : (p + 1) * pair, r] = dot_nt(kn, g_ref[r, :])
-
-    def add_key_grads(r):
-        ds = ds_ref[:, r]
-        acc_ref[:, :latent] += dot_nn(ds, q_ref[r, :]) + dot_nn(prob_ref[:, r], g_ref[r, :])
-        acc_ref[:, latent : latent + rope] += dot_nn(ds, qr_ref[r, :])
+            top_ref[8 * phase : 8 * phase + 8, r] = top
+            dp_ref[first * keys : first * keys + here, r] = dot_nt(kn, g_ref[r, :])
+
+    def add_key_grads(first, count, r):
+        mine = slice(first * keys, (first + count) * keys)
+        ds = ds_ref[mine, r]
+        acc_ref[mine, :latent] += dot_nn(ds, q_ref[r, :]) + dot_nn(prob_ref[mine, r], g_ref[r, :])
+        acc_ref[mine, latent : latent + rope] += dot_nn(ds, qr_ref[r, :])
 
     def send_pieces(kind, target):
         out = []
@@ -219,7 +219,7 @@
         return block.reshape(n_hg, piece, block.shape[1]).astype(dk_out.dtype)
 
     def one_of_last(which):
-        return acc_ref[pl.ds(pl.multiple_of(pair + which * keys, keys), keys), :]
+        return acc_ref[pl.ds(pl.multiple_of((2 + which) * keys, keys), keys), :]
 
     def folded(a):
         return jnp.sum(a.reshape(a.shape[0] // 8, 8, a.shape[1]), axis=0)
@@ -243,9 +243,7 @@
                 prob_ref[k : k + chunk, r] = (e * inv).astype(jnp.bfloat16)
                 ds = (e * scaled) * (dp_ref[k : k + chunk, r] - delta)
                 ds_ref[k : k + chunk, r] = ds.astype(jnp.bfloat16)
-        if start > 0:
-            add_key_grads(slice(start - tile, start))
-    add_key_grads(slice(rows - tile, rows))
+        add_key_grads(2, 2, slice(start, start + tile))
     comb_out[...] = one_of_last(core).astype(comb_out.dtype)
     combine = pltpu.make_async_remote_copy(
         src_ref=comb_out,
@@ -259,11 +257,16 @@
     dk_out[2] = split(one_of_last(1 - core))
     moving = send_pieces(2, lax.rem(c + n_ctx - 3 + 2 * core, n_ctx))
 
+    for start in range(0, rows, 2 * tile):
+        add_key_grads(1, 1, slice(start, start + 2 * tile))
+    combine.wait_recv()
+    dk_out[1] = split(acc_ref[keys : 2 * keys, :] + comb_in[...].astype(jnp.float32))
+    moving += send_pieces(1, behind)
+
+    for start in range(0, rows, 2 * tile):
+        add_key_grads(0, 1, slice(start, start + 2 * tile))
     dk_out[0] = split(acc_ref[:keys, :])
     moving += send_pieces(0, c)
-    combine.wait_recv()
-    dk_out[1] = split(acc_ref[keys:pair, :] + comb_in[...].astype(jnp.float32))
-    moving += send_pieces(1, behind)
 
     stores = []
     for i in range(tiles):
@@ -351,7 +354,7 @@
             pltpu.VMEM((WINDOW * tokens, rows), f32),
             pltpu.VMEM((WINDOW * tokens, rows), bf16),
             pltpu.VMEM((WINDOW * tokens, rows), bf16),
-            pltpu.VMEM((8 * PAIRS, rows), f32),
+            pltpu.VMEM((8 * len(PHASES), rows), f32),
             pltpu.VMEM((WINDOW * tokens, width), f32),
             pltpu.VMEM((tokens, width), bf16),
             pltpu.VMEM((tokens, width), bf16),

time: 30.8 us -> 30.4 us (0.987)
    pallas_call x1, Pallas kernels: 27.3 us -> 27 us  [on_device(): pl.pallas_call(functools.partial(kernel, n_ctx, n_hg), out_shape=(jax.Sha...]
where the time goes in v6:
time: 30.4 us; the launch traced here: 30.2 us
  Pallas kernels  29.6 us (97%)
  between operations  0.64 us (2%)
    pallas_call x1, Pallas kernels, on_device(): pl.pallas_call(functools.partial(kernel, n_ctx, n_hg), out_shape=(jax.Sha...  27 us
    pallas_call x1, Pallas kernels, on_device(): pl.pallas_call(hand_over, out_shape=tuple((jax.ShapeDtypeStruct(a.shape,...  2.6 us

profile of v6, /device:TPU:0, one launch (start us, length us, event | category | flops | bytes accessed | tf_op | source)
XLA Modules:
  0.0 30.2 jit_solution(5240261088997206413)
XLA Ops:
  0.6 27.0 %shard_map.93 = (bf16[2048,512]{1,0:T(8,128)(2,1)}, bf16[16,64,128]{2,1,0:T(8,128)(2,1)}, f32[64,512]{1,0:T(8,128)}, f32[64,64]{1,0:T(8,128)}) custom-call(s32[32,32]{1,0:T(8,128)} %mask_ref.1, bf16[2048,512]{1,0:T(8,128)(2,1)} %bitcast.6, bf16[16,64,128]{2,1,0:T(8,128)(2,1)} %bitcast.8, bf16[128,512]{1,0:T(8,128)(2,1)} %kn_hbm.1, bf16[64,128]{1,0:T(8,128)(2,1)} %bitcast.9, ...), custom_call_target="tpu_custom_call" | custom-call | tf_op jit(solution)/shard_map/pallas_call | solution.py:331
  27.6 2.6 %shard_map.94 = (bf16[2048,512]{1,0:T(8,128)(2,1)}, bf16[16,64,128]{2,1,0:T(8,128)(2,1)}, f32[64,512]{1,0:T(8,128)}, f32[64,64]{1,0:T(8,128)}) custom-call(bf16[2048,512]{1,0:T(8,128)(2,1)} %get-tuple-element.12.dq_in, bf16[16,64,128]{2,1,0:T(8,128)(2,1)} %get-tuple-element.13.dqr_in, f32[64,512]{1,0:T(8,128)} %get-tuple-element.14.dkn_in, ...), custom_call_target="tpu_custom_call" | custom-call | tf_op jit(solution)/shard_map/pallas_call | solution.py:376
